TPU v7x, 128 devices: a whole 4x4x4 slice. The times are simulated.
128 devices in a mesh: rep: 4 (over x), space: 32 (over z, y, core).
Axes of the slice: x: 4, y: 4, z: 4, core: 2. Of those that a mesh axis runs over, the one named last changes fastest.
Arguments:
- latents: bfloat16 [512, 512, 256], P(('rep', 'space')), may hold values from -6 to 6
- cotangent: bfloat16 [512, 512, 256], P(('rep', 'space')), may hold values from -6 to 6
- w_up: bfloat16 [2, 256, 1024], replicated, may hold values from -0.375 to 0.375
- w_down: bfloat16 [2, 1024, 256], replicated, may hold values from -0.1875 to 0.1875
- depth_w: float32 [2, 7, 256], replicated, may hold values from -2 to 2
- time_table: float32 [1000, 256], replicated, may hold values from -6 to 6
- timesteps: int32 [4], P('rep'), may hold values from 0 to 999
- brick_counts: int32 [128], P(('rep', 'space')), may hold values from 1 to 4, as said below
- send_list: int32 [128, 2, 2], P(('rep', 'space')), may hold values from 0 to 13, as said below
- recv_list: int32 [512, 4], P(('rep', 'space')), may hold values from 0 to 20, as said below
Outputs:
- d_latents: bfloat16 [512, 512, 256], P(('rep', 'space'))
- grad_up: float32 [2, 256, 1024], P(None, None, 'rep')
- grad_down: float32 [2, 1024, 256], P(None, 'rep')
- grad_depth: float32 [2, 7, 256], P(None, None, 'rep')
Inputs may be any that keep to these rules, and one draw needn't show every extreme that they name: `brick_counts`: some device of every scene holds 4 bricks and some holds one. `send_list`: entry 4 s + f names face f of local slot s; list 0 goes to the device below along space, list 1 to the device above. `recv_list`: 0 means no neighbour, 1 + 4 s + f face f of local slot s, 17 + e entry e received from the device below, 19 + e entry e from the device above. Empty slots have 0 on every side. Whenever a slot names a face across a side, the brick of that face names this slot's facing face across the opposite side.
All inputs are finite; a program needn't handle non-finite values.
Results may differ from a plain program's by a relative error of at most 0.035.
Values may be sent and summed in bfloat16 or wider, within the bound.
A program may use at most 128 MiB of HBM per device.

v0:
```python
import math

import jax
import jax.numpy as jnp
from jax import lax
from jax.sharding import PartitionSpec as P

E = 8


CUBIC = 0.044715
ROOT = math.sqrt(2.0 / math.pi)
FORWARD_ORDER = (0, 1, 2, 3, 4, 5, 6)
MIRROR_ORDER = (0, 2, 1, 4, 3, 6, 5)


def from_behind(value, axis, steps):
    count = lax.axis_size(axis)
    initial, last = (max(0, -steps), min(count, count - steps))
    return lax.ppermute(value, axis, [(source, source + steps) for source in range(initial, last)])


def gelu_tanh(values):
    return 0.5 * values * (1.0 + jnp.tanh(ROOT * (values + CUBIC * values * values * values)))


def gelu_slope(values):
    inner = jnp.tanh(ROOT * (values + CUBIC * values * values * values))
    return 0.5 * (1.0 + inner) + 0.5 * values * (1.0 - inner * inner) * ROOT * (
        1.0 + 3.0 * CUBIC * values * values
    )


def planes_of(fields):
    count = fields.shape[0]
    cube = fields.reshape(count, E, E, E, fields.shape[-1])
    stacked = jnp.stack([cube[:, 0], cube[:, E - 1], cube[:, :, 0], cube[:, :, E - 1]], axis=1)
    return stacked.reshape(count * 4, E * E, fields.shape[-1])


def neighbours(field, ghosts):
    count = field.shape[0]
    width = field.shape[-1]
    cube = field.reshape(count, E, E, E, width).astype(jnp.float32)
    sides = ghosts.reshape(count, 4, E, E, width).astype(jnp.float32)
    along_x = jnp.concatenate([sides[:, 0:1], cube, sides[:, 1:2]], axis=1)
    along_y = jnp.concatenate([sides[:, 2][:, :, None], cube, sides[:, 3][:, :, None]], axis=2)
    along_z = jnp.pad(cube, ((0, 0), (0, 0), (0, 0), (1, 1), (0, 0)))
    pieces = [
        cube,
        along_x[:, :-2],
        along_x[:, 2:],
        along_y[:, :, :-2],
        along_y[:, :, 2:],
        along_z[:, :, :, :-2],
        along_z[:, :, :, 2:],
    ]
    return [piece.reshape(-1, width) for piece in pieces]


def combine(fields, weights, order):
    total = weights[order[0]][None, :] * fields[0]
    for index in range(1, 7):
        total = total + weights[order[index]][None, :] * fields[index]
    return total


def trade_faces(fields, sends, recvs):
    copies, bricks, voxels, channels = fields.shape
    planes = planes_of(fields.reshape(copies * bricks, voxels, channels)).reshape(
        copies, bricks * 4, E * E, channels
    )
    outgoing = planes[:, sends.reshape(-1)].reshape(copies, 2, sends.shape[1], E * E, channels)
    from_lower = from_behind(outgoing[:, 1], "space", 1)
    from_upper = from_behind(outgoing[:, 0], "space", -1)
    blank = jnp.zeros((copies, 1, E * E, channels), jnp.bfloat16)
    face_pool = jnp.concatenate([blank, planes, from_lower, from_upper], axis=1)
    return face_pool[:, recvs.reshape(-1)].reshape(copies, bricks, 4, E * E, channels)


def on_device(
    latents,
    cotangent,
    w_up,
    w_down,
    depth_w,
    time_table,
    timesteps,
    brick_counts,
    send_list,
    recv_list,
):
    bricks, voxels, channels = latents.shape
    blocks = w_up.shape[0]
    sends = send_list[0]
    occupied = (jnp.arange(bricks, dtype=jnp.int32) < brick_counts[0]).astype(jnp.float32)[
        :, None, None
    ]
    time_shift = time_table[timesteps[0]]
    field = (latents.astype(jnp.float32) * occupied).astype(jnp.bfloat16)
    saved = []
    for block in range(blocks):
        ghosts = trade_faces(field[None], sends, recv_list)[0]
        near = neighbours(field, ghosts)
        activation = (combine(near, depth_w[block], FORWARD_ORDER) + time_shift[None, :]).astype(
            jnp.bfloat16
        )
        preact = jnp.dot(activation, w_up[block], preferred_element_type=jnp.float32)
        hidden = gelu_tanh(preact).astype(jnp.bfloat16)
        summed = field.reshape(-1, channels).astype(jnp.float32) + jnp.dot(
            hidden, w_down[block], preferred_element_type=jnp.float32
        )
        saved.append((field, ghosts, activation, preact, hidden))
        field = (summed.reshape(bricks, voxels, channels) * occupied).astype(jnp.bfloat16)
    grad = (cotangent.astype(jnp.float32) * occupied).astype(jnp.bfloat16)
    parts_up = [None] * blocks
    parts_down = [None] * blocks
    parts_depth = [None] * blocks
    contract_rows = (((0,), (0,)), ((), ()))
    contract_cols = (((1,), (1,)), ((), ()))
    for block in range(blocks - 1, -1, -1):
        field_in, ghosts_in, activation, preact, hidden = saved[block]
        flat_grad = grad.reshape(-1, channels)
        parts_down[block] = lax.dot_general(
            hidden, flat_grad, contract_rows, preferred_element_type=jnp.float32
        )
        d_hidden = lax.dot_general(
            flat_grad, w_down[block], contract_cols, preferred_element_type=jnp.float32
        )
        d_preact = (d_hidden * gelu_slope(preact)).astype(jnp.bfloat16)
        parts_up[block] = lax.dot_general(
            activation, d_preact, contract_rows, preferred_element_type=jnp.float32
        )
        d_act = lax.dot_general(
            d_preact, w_up[block], contract_cols, preferred_element_type=jnp.float32
        ).astype(jnp.bfloat16)
        d_field = d_act.reshape(bricks, voxels, channels)
        ghosts_grad = trade_faces(d_field[None], sends, recv_list)[0]
        near_in = neighbours(field_in, ghosts_in)
        d_wide = d_act.astype(jnp.float32)
        parts_depth[block] = jnp.stack([jnp.sum(piece * d_wide, axis=0) for piece in near_in])
        back = combine(neighbours(d_field, ghosts_grad), depth_w[block], MIRROR_ORDER)
        total = flat_grad.astype(jnp.float32) + back
        grad = (total.reshape(bricks, voxels, channels) * occupied).astype(jnp.bfloat16)
    local_up = jnp.stack(parts_up)
    local_down = jnp.stack(parts_down)
    local_depth = jnp.stack(parts_depth)
    whole = (
        lax.psum(local_up.astype(jnp.bfloat16), "space").astype(jnp.float32),
        lax.psum(local_down.astype(jnp.bfloat16), "space").astype(jnp.float32),
        lax.psum(local_depth.astype(jnp.bfloat16), "space").astype(jnp.float32),
    )
    sum_up, sum_down, sum_depth = (
        lax.psum_scatter(
            whole[0].astype(jnp.bfloat16), "rep", scatter_dimension=2, tiled=True
        ).astype(jnp.float32),
        lax.psum_scatter(
            whole[1].astype(jnp.bfloat16), "rep", scatter_dimension=1, tiled=True
        ).astype(jnp.float32),
        lax.psum_scatter(
            whole[2].astype(jnp.bfloat16), "rep", scatter_dimension=2, tiled=True
        ).astype(jnp.float32),
    )
    scale = 1.0 / math.sqrt(bricks * lax.axis_size("rep") * lax.axis_size("space") * voxels)
    return (grad, sum_up * scale, sum_down * scale, sum_depth * scale)


def solution(mesh):
    return jax.shard_map(
        on_device,
        mesh=mesh,
        in_specs=(
            P(("rep", "space"), None, None),
            P(("rep", "space"), None, None),
            P(),
            P(),
            P(),
            P(),
            P("rep"),
            P(("rep", "space")),
            P(("rep", "space"), None, None),
            P(("rep", "space"), None),
        ),
        out_specs=(
            P(("rep", "space"), None, None),
            P(None, None, "rep"),
            P(None, "rep", None),
            P(None, None, "rep"),
        ),
        check_vma=False,
    )
```

profile of v0, /device:TPU:1, one launch (start us, length us, event | category | flops | bytes accessed | tf_op | source)
XLA Modules:
  0.0 312.6 jit_solution(17737770641990076478)
XLA Ops:
  8.0 3.4 %multiply_convert_fusion.6 = (bf16[4,512,256]{2,1,0:T(8,128)(2,1)}, bf16[4,512,256]{2,1,0:T(8,128)(2,1)S(1)}) fusion(bf16[4,512,256]{2,1,0:T(8,128)(2,1)} %param.11, f32[4]{0:T(128)S(1)} %compare_convert_fusion, bf16[4,512,256]{2,1,0:T(8,128)(2,1)} %param.10), kind=kLoop, calls=%fused_computation.163 | loop fusion | flops 3145728 | bytes 4194320 | tf_op jit(solution)/shard_map/convert_element_type | solution.py:115
  12.3 4.6 %collective-permute-start = (bf16[1,2,64,256]{3,2,1,0:T(8,128)(2,1)S(1)}, bf16[1,2,64,256]{3,2,1,0:T(8,128)(2,1)S(1)}, u32[]{:S(2)}, u32[]{:S(2)}) collective-permute-start(bf16[1,2,64,256]{3,2,1,0:T(8,128)(2,1)S(1)} %get-tuple-element.97), channel_id=1, source_target_pairs={{0,1},{1,2},{2,3},{3,4},{4,5},{5,6},{6,7},{7,8},{8,9},{9,10},{10,1... | collective-permute-start | bytes 196616 | tf_op jit(solution)/shard_map/ppermute | solution.py:20
  16.9 1.9 collective-permute-start.1
  18.8 1.6 convert_element_type.165
  21.3 1.2 collective-permute-done.1
  23.4 1.4 copy-done.22
  24.8 1.4 pad_maximum_fusion.15
  26.3 1.2 fusion.63
  30.8 1.3 fusion.81
  32.3 3.0 convolution_add_fusion
  35.4 1.8 fusion.97
  37.8 2.5 collective-permute-start.2
  40.3 2.1 collective-permute-start.3
  42.6 3.2 %collective-permute-done.3 = bf16[1,2,64,256]{3,2,1,0:T(8,128)(2,1)S(1)} collective-permute-done((bf16[1,2,64,256]{3,2,1,0:T(8,128)(2,1)S(1)}, bf16[1,2,64,256]{3,2,1,0:T(8,128)(2,1)S(1)}, u32[]{:S(2)}, u32[]{:S(2)}) %collective-permute-start.3) | collective-permute-done | bytes 65568 | tf_op jit(solution)/shard_map/ppermute | solution.py:20
  45.8 1.0 maximum_bitcast_fusion.1
  46.8 1.7 gather_fusion.3
  48.7 1.4 copy-done.21
  50.1 1.7 pad_maximum_fusion.11
  53.6 2.2 fusion.22
  55.9 1.3 fusion.76
  57.8 5.9 %fusion.8 = bf16[2048,1024]{1,0:T(8,128)(2,1)S(1)} fusion(f32[2048,1024]{1,0:T(8,128)S(1)} %fusion.76, bf16[2048,256]{1,0:T(8,128)(2,1)S(1)} %bitcast.382, bf16[2,1024,256]{2,1,0:T(8,128)(2,1)S(1)} %copy-done.41), kind=kOutput, calls=%fused_computation.20 | convolution fusion | flops 1113587712 | bytes 14155776 | tf_op jit(solution)/shard_map/dot_general | solution.py:127
  63.7 4.2 %fusion.38 = (bf16[256]{0:T(256)(128)(2,1)S(1)}, bf16[256]{0:T(256)(128)(2,1)S(1)}, bf16[256]{0:T(256)(128)(2,1)S(1)}, bf16[256]{0:T(256)(128)(2,1)S(1)}, bf16[2...) fusion(f32[4,8,8,8,256]{4,3,2,1,0:T(8,128)S(1)} %copy.124, ...), kind=kOutput, calls=%fused_computation.80 | convolution fusion | flops 1083701504 | bytes 20459008 | tf_op jit(solution)/shard_map/dot_general | solution.py:134
  69.7 1.9 collective-permute-start.4
  71.6 2.8 collective-permute-start.5
  74.4 6.1 %fusion.71 = bf16[1,1024,256]{2,1,0:T(8,128)(2,1)} fusion(bf16[2048,256]{1,0:T(8,128)(2,1)S(1)} %bitcast.383, f32[2048,1024]{1,0:T(8,128)} %copy-done.3), kind=kOutput, calls=%fused_computation.168 | convolution fusion | flops 1092878336 | bytes 9961472 | tf_op jit(solution)/shard_map/dot_general | solution.py:124
  80.5 1.6 convert_element_type.181
  83.2 1.7 gather_fusion.5
  85.1 1.4 copy-done.23
  86.5 1.7 pad_maximum_fusion.7
  88.2 2.2 fusion.31
  90.5 3.6 %fusion.74 = bf16[1,1024,256]{2,1,0:T(8,128)(2,1)S(1)} fusion(bf16[2048,256]{1,0:T(8,128)(2,1)S(1)} %fusion.31, f32[2048,1024]{1,0:T(8,128)S(1)} %bitcast.361), kind=kOutput, calls=%fused_computation.171 | convolution fusion | flops 1092878336 | bytes 9961472 | tf_op jit(solution)/shard_map/dot_general | solution.py:124
  94.2 5.9 %fusion.13 = bf16[2048,1024]{1,0:T(8,128)(2,1)S(1)} fusion(f32[2048,1024]{1,0:T(8,128)S(1)} %bitcast.361, bf16[2048,256]{1,0:T(8,128)(2,1)S(1)} %fusion.31, bf16[2,1024,256]{2,1,0:T(8,128)(2,1)S(1)} %copy-done.42), kind=kOutput, calls=%fused_computation.25 | convolution fusion | flops 1113587712 | bytes 14155776 | tf_op jit(solution)/shard_map/dot_general | solution.py:127
  100.2 5.9 %fusion.52 = (bf16[256]{0:T(256)(128)(2,1)S(1)}, bf16[256]{0:T(256)(128)(2,1)S(1)}, bf16[256]{0:T(256)(128)(2,1)S(1)}, bf16[256]{0:T(256)(128)(2,1)S(1)}, bf16[2...) fusion(f32[4,8,8,8,256]{4,3,2,1,0:T(8,128)S(1)} %copy-done.12, ...), kind=kOutput, calls=%fused_computation.94 | convolution fusion | flops 1090517248 | bytes 20459008 | tf_op jit(solution)/shard_map/dot_general | solution.py:134
  107.2 1.1 pad_maximum_fusion.17
  108.4 4.3 %fusion.73 = bf16[1,256,1024]{2,1,0:T(8,128)(2,1)} fusion(bf16[2048,256]{1,0:T(8,128)(2,1)S(1)} %copy-done.27, bf16[2048,1024]{1,0:T(8,128)(2,1)} %copy-done.32), kind=kOutput, calls=%fused_computation.170 | convolution fusion | flops 1074003968 | bytes 5767168 | tf_op jit(solution)/shard_map/dot_general | solution.py:131
  113.7 3.1 %collective-permute-start.6 = (bf16[1,2,64,256]{3,2,1,0:T(8,128)(2,1)S(1)}, bf16[1,2,64,256]{3,2,1,0:T(8,128)(2,1)S(1)}, u32[]{:S(2)}, u32[]{:S(2)}) collective-permute-start(bf16[1,2,64,256]{3,2,1,0:T(8,128)(2,1)S(1)} %get-tuple-element.91), channel_id=1, source_target_pairs={{0,1},{1,2},{2,3},{3,4},{4,5},{5,6},{6,7},{7,8},{8,9},{9,10},{10,1... | collective-permute-start | bytes 196616 | tf_op jit(solution)/shard_map/ppermute | solution.py:20
  116.9 2.2 collective-permute-start.7
  119.1 3.8 %fusion.72 = bf16[1,256,1024]{2,1,0:T(8,128)(2,1)S(1)} fusion(bf16[2048,256]{1,0:T(8,128)(2,1)} %get-tuple-element.34, bf16[2048,1024]{1,0:T(8,128)(2,1)} %copy-done.44), kind=kOutput, calls=%fused_computation.169 | convolution fusion | flops 1074003968 | bytes 5767168 | tf_op jit(solution)/shard_map/dot_general | solution.py:131
  122.9 1.1 pad_maximum_fusion.16
  124.1 6.8 %reduce-scatter.10.cloned.1.call-done = bf16[64,14]{1,0:T(8,128)(2,1)} async-done(((bf16[256,14]{1,0:T(8,128)(2,1)}), bf16[64,14]{1,0:T(8,128)(2,1)}) %reduce-scatter.10.cloned.1.call-update) | async-done | bytes 1808
  131.7 65.2 %psum.26 = bf16[2,7,64]{2,1,0:T(8,128)(2,1)S(1)} all-reduce(bf16[2,7,64]{2,1,0:T(8,128)(2,1)S(1)} %copy.135), channel_id=1, replica_groups=mesh['rep'=4,'space'=32] {'space'}, use_global_device_ids=true, to_apply=%region_18.19 | all-reduce | flops 896 | bytes 3584 | tf_op jit(solution)/shard_map/psum | solution.py:151
  197.5 1.0 maximum_bitcast_fusion.3
  198.5 1.7 gather_fusion.7
  200.4 1.4 pad_maximum_fusion.3
  201.9 1.1 fusion.45
  203.1 1.3 multiply_convert_fusion.3
  204.4 99.6 %all-reduce.7.cloned.1.call-done = (bf16[2,256,256]{2,1,0:T(8,128)(2,1)}, bf16[2,256,256]{2,1,0:T(8,128)(2,1)}) async-done(((bf16[2,256,256]{2,1,0:T(8,128)(2,1)}, bf16[2,256,256]{2,1,0:T(8,128)(2,1)}), (bf16[2,256,256]{2,1,0:T(8,128)(2,1)}, bf16[2,256,256]{2,1,0:T(8,128)(2,1)})) %all-reduce.7.cloned.1.call-update) | async-done | bytes 524304 | tf_op jit(solution)/shard_map/psum | solution.py:149
  304.0 2.1 convert_multiply_fusion.17
  (188 shorter events, 15.9 us)
Async XLA Ops:
  7.2 14.1 %copy-start = (f32[1000,256]{1,0:T(8,128)S(1)}, f32[1000,256]{1,0:T(8,128)}, u32[]{:S(2)}) copy-start(f32[1000,256]{1,0:T(8,128)} %param.15) | copy-start | bytes 3072004
  7.2 123.6 %reduce-scatter.10.cloned.1.call-start = ((), (), s32[]{:S(2)}) async-start(), calls=%async_computation.5 | async-start | bytes 81920
  8.0 3.5 %copy-start.43 = (s32[1,2,2]{2,1,0:T(2,128)S(1)}, s32[1,2,2]{2,1,0:T(2,128)}, u32[]{:S(2)}) copy-start(s32[1,2,2]{2,1,0:T(2,128)} %param.18) | copy-start | bytes 52
  11.4 14.9 %copy-start.4 = (bf16[4,512,256]{2,1,0:T(8,128)(2,1)}, bf16[4,512,256]{2,1,0:T(8,128)(2,1)S(1)}, u32[]{:S(2)}) copy-start(bf16[4,512,256]{2,1,0:T(8,128)(2,1)S(1)} %get-tuple-element.114) | copy-start | bytes 3145732
  11.7 9.4 %copy-start.39 = (s32[4,4]{1,0:T(4,128)S(1)}, s32[4,4]{1,0:T(4,128)}, u32[]{:S(2)}) copy-start(s32[4,4]{1,0:T(4,128)} %param.19) | copy-start | bytes 196
  11.7 9.5 %copy-start.38 = (f32[2,7,256]{2,0,1:T(2,128)S(1)}, f32[2,7,256]{2,0,1:T(2,128)}, u32[]{:S(2)}) copy-start(f32[2,7,256]{2,0,1:T(2,128)} %param.14) | copy-start | bytes 43012
  12.3 9.0 %collective-permute-start = (bf16[1,2,64,256]{3,2,1,0:T(8,128)(2,1)S(1)}, bf16[1,2,64,256]{3,2,1,0:T(8,128)(2,1)S(1)}, u32[]{:S(2)}, u32[]{:S(2)}) collective-permute-start(bf16[1,2,64,256]{3,2,1,0:T(8,128)(2,1)S(1)} %get-tuple-element.97), channel_id=1, source_target_pairs={{0,1},{1,2},{2,3},{3,4},{4,5},{5,6},{6,7},{7,8},{8,9},{9,10},{10,1... | collective-permute-start | bytes 196616 | tf_op jit(solution)/shard_map/ppermute | solution.py:20
  16.9 5.6 %collective-permute-start.1 = (bf16[1,2,64,256]{3,2,1,0:T(8,128)(2,1)S(1)}, bf16[1,2,64,256]{3,2,1,0:T(8,128)(2,1)S(1)}, u32[]{:S(2)}, u32[]{:S(2)}) collective-permute-start(bf16[1,2,64,256]{3,2,1,0:T(8,128)(2,1)S(1)} %get-tuple-element.98), channel_id=1, source_target_pairs={{1,0},{2,1},{3,2},{4,3},{5,4},{6,5},{7,6},{8,7},{9,8},{10,9},{11,1... | collective-permute-start | bytes 196616 | tf_op jit(solution)/shard_map/ppermute | solution.py:20
  26.2 2.0 copy-start.11
  26.2 2.6 copy-start.13
  26.2 3.3 %copy-start.15 = (f32[4,8,8,8,256]{4,3,2,1,0:T(8,128)}, f32[4,8,8,8,256]{4,3,2,1,0:T(8,128)S(1)}, u32[]{:S(2)}) copy-start(f32[4,8,8,8,256]{4,3,2,1,0:T(8,128)S(1)} %get-tuple-element.56) | copy-start | bytes 6291460
  26.3 3.9 %copy-start.17 = (f32[4,8,8,8,256]{4,3,2,1,0:T(8,128)}, f32[4,8,8,8,256]{4,3,2,1,0:T(8,128)S(1)}, u32[]{:S(2)}) copy-start(f32[4,8,8,8,256]{4,3,2,1,0:T(8,128)S(1)} %get-tuple-element.57) | copy-start | bytes 6291460
  26.3 4.5 %copy-start.19 = (f32[4,8,8,8,256]{4,3,2,1,0:T(8,128)}, f32[4,8,8,8,256]{4,3,2,1,0:T(8,128)S(1)}, u32[]{:S(2)}) copy-start(f32[4,8,8,8,256]{4,3,2,1,0:T(8,128)S(1)} %get-tuple-element.58) | copy-start | bytes 6291460
  26.3 4.5 %copy-start.33 = (bf16[2,256,1024]{2,1,0:T(8,128)(2,1)S(1)}, bf16[2,256,1024]{2,1,0:T(8,128)(2,1)}, u32[]{:S(2)}) copy-start(bf16[2,256,1024]{2,1,0:T(8,128)(2,1)} %param.12) | copy-start | bytes 3145732
  32.1 3.3 %copy-start.2 = (f32[2048,1024]{1,0:T(8,128)}, f32[2048,1024]{1,0:T(8,128)S(1)}, u32[]{:S(2)}) copy-start(f32[2048,1024]{1,0:T(8,128)S(1)} %fusion.81) | copy-start | bytes 25165828
  37.8 4.8 %collective-permute-start.2 = (bf16[1,2,64,256]{3,2,1,0:T(8,128)(2,1)S(1)}, bf16[1,2,64,256]{3,2,1,0:T(8,128)(2,1)S(1)}, u32[]{:S(2)}, u32[]{:S(2)}) collective-permute-start(bf16[1,2,64,256]{3,2,1,0:T(8,128)(2,1)S(1)} %get-tuple-element.95), channel_id=1, source_target_pairs={{0,1},{1,2},{2,3},{3,4},{4,5},{5,6},{6,7},{7,8},{8,9},{9,10},{10,1... | collective-permute-start | bytes 196616 | tf_op jit(solution)/shard_map/ppermute | solution.py:20
  40.3 5.6 %collective-permute-start.3 = (bf16[1,2,64,256]{3,2,1,0:T(8,128)(2,1)S(1)}, bf16[1,2,64,256]{3,2,1,0:T(8,128)(2,1)S(1)}, u32[]{:S(2)}, u32[]{:S(2)}) collective-permute-start(bf16[1,2,64,256]{3,2,1,0:T(8,128)(2,1)S(1)} %get-tuple-element.96), channel_id=1, source_target_pairs={{1,0},{2,1},{3,2},{4,3},{5,4},{6,5},{7,6},{8,7},{9,8},{10,9},{11,1... | collective-permute-start | bytes 196616 | tf_op jit(solution)/shard_map/ppermute | solution.py:20
  53.6 2.2 copy-start.34
  55.9 1.9 copy-start.41
  57.2 6.5 %copy-start.3 = (f32[2048,1024]{1,0:T(8,128)}, f32[2048,1024]{1,0:T(8,128)S(1)}, u32[]{:S(2)}) copy-start(f32[2048,1024]{1,0:T(8,128)S(1)} %fusion.76) | copy-start | bytes 25165828
  63.7 4.3 %copy-start.32 = (bf16[2048,1024]{1,0:T(8,128)(2,1)}, bf16[2048,1024]{1,0:T(8,128)(2,1)S(1)}, u32[]{:S(2)}) copy-start(bf16[2048,1024]{1,0:T(8,128)(2,1)S(1)} %fusion.8) | copy-start | bytes 12582916
  68.0 6.4 %copy-start.29 = (bf16[4,512,256]{2,1,0:T(8,128)(2,1)S(1)}, bf16[4,512,256]{2,1,0:T(8,128)(2,1)}, u32[]{:S(2)}) copy-start(bf16[4,512,256]{2,1,0:T(8,128)(2,1)} %get-tuple-element.113) | copy-start | bytes 3145732
  69.7 12.5 %collective-permute-start.4 = (bf16[1,2,64,256]{3,2,1,0:T(8,128)(2,1)S(1)}, bf16[1,2,64,256]{3,2,1,0:T(8,128)(2,1)S(1)}, u32[]{:S(2)}, u32[]{:S(2)}) collective-permute-start(bf16[1,2,64,256]{3,2,1,0:T(8,128)(2,1)S(1)} %get-tuple-element.93), channel_id=1, source_target_pairs={{0,1},{1,2},{2,3},{3,4},{4,5},{5,6},{6,7},{7,8},{8,9},{9,10},{10,1... | collective-permute-start | bytes 196616 | tf_op jit(solution)/shard_map/ppermute | solution.py:20
  71.6 8.9 %copy-start.8 = (bf16[2048,256]{1,0:T(8,128)(2,1)S(1)}, bf16[2048,256]{1,0:T(8,128)(2,1)}, u32[]{:S(2)}) copy-start(bf16[2048,256]{1,0:T(8,128)(2,1)} %copy-done.7) | copy-start | bytes 3145732
  71.6 10.5 %collective-permute-start.5 = (bf16[1,2,64,256]{3,2,1,0:T(8,128)(2,1)S(1)}, bf16[1,2,64,256]{3,2,1,0:T(8,128)(2,1)S(1)}, u32[]{:S(2)}, u32[]{:S(2)}) collective-permute-start(bf16[1,2,64,256]{3,2,1,0:T(8,128)(2,1)S(1)} %get-tuple-element.94), channel_id=1, source_target_pairs={{1,0},{2,1},{3,2},{4,3},{5,4},{6,5},{7,6},{8,7},{9,8},{10,9},{11,1... | collective-permute-start | bytes 196616 | tf_op jit(solution)/shard_map/ppermute | solution.py:20
  86.4 4.0 %slice-start = ((s8[8388608]{0:T(1024)(128)(4,1)}), s8[4194304]{0:T(1024)(128)(4,1)S(1)}, s32[]{:S(2)}) async-start(s8[8388608]{0:T(1024)(128)(4,1)} %bitcast.360), calls=%async_computation.7 | async-start | bytes 8388608
  88.2 2.3 slice-start.1
  90.5 3.6 %copy-start.30 = (bf16[2048,256]{1,0:T(8,128)(2,1)}, bf16[2048,256]{1,0:T(8,128)(2,1)S(1)}, u32[]{:S(2)}) copy-start(bf16[2048,256]{1,0:T(8,128)(2,1)S(1)} %fusion.31) | copy-start | bytes 3145732
  90.5 3.6 %copy-start.42 = (bf16[2,1024,256]{2,1,0:T(8,128)(2,1)S(1)}, bf16[2,1024,256]{2,1,0:T(8,128)(2,1)}, u32[]{:S(2)}) copy-start(bf16[2,1024,256]{2,1,0:T(8,128)(2,1)} %param.13) | copy-start | bytes 3145732
  94.1 6.0 %copy-start.6 = (bf16[4,512,256]{2,1,0:T(8,128)(2,1)S(1)}, bf16[4,512,256]{2,1,0:T(8,128)(2,1)}, u32[]{:S(2)}) copy-start(bf16[4,512,256]{2,1,0:T(8,128)(2,1)} %copy-done.4) | copy-start | bytes 3145732
  94.1 6.0 %copy-start.10 = (f32[4,8,8,8,256]{4,3,2,1,0:T(8,128)S(1)}, f32[4,8,8,8,256]{4,3,2,1,0:T(8,128)}, u32[]{:S(2)}) copy-start(f32[4,8,8,8,256]{4,3,2,1,0:T(8,128)} %copy-done.9) | copy-start | bytes 6291460
  94.1 6.0 %copy-start.12 = (f32[4,8,8,8,256]{4,3,2,1,0:T(8,128)S(1)}, f32[4,8,8,8,256]{4,3,2,1,0:T(8,128)}, u32[]{:S(2)}) copy-start(f32[4,8,8,8,256]{4,3,2,1,0:T(8,128)} %copy-done.11) | copy-start | bytes 6291460
  94.1 6.0 %copy-start.14 = (f32[4,8,8,8,256]{4,3,2,1,0:T(8,128)S(1)}, f32[4,8,8,8,256]{4,3,2,1,0:T(8,128)}, u32[]{:S(2)}) copy-start(f32[4,8,8,8,256]{4,3,2,1,0:T(8,128)} %copy-done.13) | copy-start | bytes 6291460
  94.1 6.0 %copy-start.16 = (f32[4,8,8,8,256]{4,3,2,1,0:T(8,128)S(1)}, f32[4,8,8,8,256]{4,3,2,1,0:T(8,128)}, u32[]{:S(2)}) copy-start(f32[4,8,8,8,256]{4,3,2,1,0:T(8,128)} %copy-done.15) | copy-start | bytes 6291460
  94.1 6.0 %copy-start.18 = (f32[4,8,8,8,256]{4,3,2,1,0:T(8,128)S(1)}, f32[4,8,8,8,256]{4,3,2,1,0:T(8,128)}, u32[]{:S(2)}) copy-start(f32[4,8,8,8,256]{4,3,2,1,0:T(8,128)} %copy-done.17) | copy-start | bytes 6291460
  94.2 6.0 %copy-start.20 = (f32[4,8,8,8,256]{4,3,2,1,0:T(8,128)S(1)}, f32[4,8,8,8,256]{4,3,2,1,0:T(8,128)}, u32[]{:S(2)}) copy-start(f32[4,8,8,8,256]{4,3,2,1,0:T(8,128)} %copy-done.19) | copy-start | bytes 6291460
  94.2 6.0 %copy-start.35 = (bf16[2,256,1024]{2,1,0:T(8,128)(2,1)S(1)}, bf16[2,256,1024]{2,1,0:T(8,128)(2,1)}, u32[]{:S(2)}) copy-start(bf16[2,256,1024]{2,1,0:T(8,128)(2,1)} %param.12) | copy-start | bytes 3145732
  100.2 5.9 %copy-start.44 = (bf16[2048,1024]{1,0:T(8,128)(2,1)}, bf16[2048,1024]{1,0:T(8,128)(2,1)S(1)}, u32[]{:S(2)}) copy-start(bf16[2048,1024]{1,0:T(8,128)(2,1)S(1)} %fusion.13) | copy-start | bytes 12582916
  100.2 7.0 %copy-start.36 = (bf16[1,1024,256]{2,1,0:T(8,128)(2,1)S(1)}, bf16[1,1024,256]{2,1,0:T(8,128)(2,1)}, u32[]{:S(2)}) copy-start(bf16[1,1024,256]{2,1,0:T(8,128)(2,1)} %fusion.71) | copy-start | bytes 1572868
  106.1 2.3 copy-start.27
  107.2 95.9 %reduce-scatter.8.cloned.1.call-start = ((), (), s32[]{:S(2)}) async-start(), calls=%async_computation.4 | async-start | bytes 1310720 | tf_op jit(solution)/shard_map/reduce_scatter | solution.py:157
  108.3 94.8 %reduce-scatter.6.cloned.1.call-start = ((), (), s32[]{:S(2)}) async-start(), calls=%async_computation.3 | async-start | bytes 1310720 | tf_op jit(solution)/shard_map/reduce_scatter | solution.py:154
  108.4 4.4 %copy-start.24 = (bf16[2048,256]{1,0:T(8,128)(2,1)S(1)}, bf16[2048,256]{1,0:T(8,128)(2,1)}, u32[]{:S(2)}) copy-start(bf16[2048,256]{1,0:T(8,128)(2,1)} %get-tuple-element.115) | copy-start | bytes 3145732
  113.7 83.8 %collective-permute-start.6 = (bf16[1,2,64,256]{3,2,1,0:T(8,128)(2,1)S(1)}, bf16[1,2,64,256]{3,2,1,0:T(8,128)(2,1)S(1)}, u32[]{:S(2)}, u32[]{:S(2)}) collective-permute-start(bf16[1,2,64,256]{3,2,1,0:T(8,128)(2,1)S(1)} %get-tuple-element.91), channel_id=1, source_target_pairs={{0,1},{1,2},{2,3},{3,4},{4,5},{5,6},{6,7},{7,8},{8,9},{9,10},{10,1... | collective-permute-start | bytes 196616 | tf_op jit(solution)/shard_map/ppermute | solution.py:20
  116.9 80.6 %collective-permute-start.7 = (bf16[1,2,64,256]{3,2,1,0:T(8,128)(2,1)S(1)}, bf16[1,2,64,256]{3,2,1,0:T(8,128)(2,1)S(1)}, u32[]{:S(2)}, u32[]{:S(2)}) collective-permute-start(bf16[1,2,64,256]{3,2,1,0:T(8,128)(2,1)S(1)} %get-tuple-element.92), channel_id=1, source_target_pairs={{1,0},{2,1},{3,2},{4,3},{5,4},{6,5},{7,6},{8,7},{9,8},{10,9},{11,1... | collective-permute-start | bytes 196616 | tf_op jit(solution)/shard_map/ppermute | solution.py:20
  119.1 3.9 %copy-start.37 = (bf16[1,256,1024]{2,1,0:T(8,128)(2,1)S(1)}, bf16[1,256,1024]{2,1,0:T(8,128)(2,1)}, u32[]{:S(2)}) copy-start(bf16[1,256,1024]{2,1,0:T(8,128)(2,1)} %fusion.73) | copy-start | bytes 1572868
  124.0 180.0 %all-reduce.7.cloned.1.call-start = ((), (), s32[]{:S(2)}) async-start(), calls=%async_computation.6 | async-start | bytes 1048576 | tf_op jit(solution)/shard_map/psum | solution.py:149
  203.1 103.0 %copy-start.1 = (f32[1000,256]{1,0:T(8,128)S(1)}, f32[1000,256]{1,0:T(8,128)}, u32[]{:S(2)}) copy-start(f32[1000,256]{1,0:T(8,128)} %param.15) | copy-start | bytes 3072004
  (11 other events, 15.9 us)
Sparse Core Ops, SparseCore 0:
  107.3 23.4 reduce-scatter.9
  133.3 24.0 reduce-scatter.7
  160.4 23.1 reduce-scatter.5
  203.2 100.7 all-reduce.6
where the time goes:
time: 314 us; the launch traced here: 313 us
  waiting for transfers between devices  111 us (35%)
  blocking collectives  65.2 us (21%)
  matrix products  45.3 us (14%)
  other arithmetic  31 us (10%)
  local copies, waits for them, and re-layouts  22.7 us (7%)
  starting transfers between devices  21.2 us (7%)
  between operations  16.4 us (5%)
    psum x1, waiting for transfers between devices, on_device(): lax.psum(local_up.astype(jnp.bfloat16), 'space').astype(jnp.float32)  99.6 us
    psum x1, blocking collectives, on_device(): lax.psum(local_depth.astype(jnp.bfloat16), 'space').astype(jnp.float32)  65.2 us
    ppermute x8, starting transfers between devices, from_behind(): lax.ppermute(value, axis, [(source, source + steps) for source in range(i...  21.1 us
    unnamed x102, local copies, waits for them, and re-layouts  12.1 us
    dot_general x2, matrix products, on_device(): lax.dot_general(flat_grad, w_down[block], contract_cols, preferred_elemen...  11.8 us
    dot_general x2, matrix products, on_device(): lax.dot_general(d_preact, w_up[block], contract_cols, preferred_element_t...  10.1 us
    dot_general x2, matrix products, on_device(): lax.dot_general(hidden, flat_grad, contract_rows, preferred_element_type=...  9.67 us
    dot_general x2, matrix products, on_device(): lax.dot_general(activation, d_preact, contract_rows, preferred_element_ty...  8.18 us
  transfers between devices with their start and end apart: 12, of which 4 were waited for; matrix products, arithmetic and copies ran while one was open for 9% of the time, Pallas kernels for 0%

commit v1 on v0

v1 whole, which is shorter than its diff:
```python
import functools
import math

import jax
import jax.numpy as jnp
from jax import lax
from jax.experimental import pallas as pl
from jax.experimental.pallas import tpu as pltpu
from jax.sharding import PartitionSpec as P

MESH = pl.DeviceIdType.MESH
BF = jnp.bfloat16
F32 = jnp.float32
CUBIC = 0.044715
ROOT = math.sqrt(2.0 / math.pi)
NT = (((1,), (1,)), ((), ()))


def gelu_pair(u):
    square = u * u
    gate = 0.5 + 0.5 * jnp.tanh(u * (ROOT + (ROOT * CUBIC) * square))
    hidden = u * gate
    slope = gate + hidden * (1.0 - gate) * (2.0 * ROOT + (6.0 * ROOT * CUBIC) * square)
    return hidden, slope


def dot(a, b):
    return jnp.dot(a, b, preferred_element_type=F32)


def dot_nt(a, b):
    return lax.dot_general(a, b, NT, preferred_element_type=F32)


def kernel(
    scale,
    lat_hbm, cot_hbm, wu_hbm, wd_hbm, dw_ref, tt_hbm, ts_ref, cnt_ref, snd_ref, rcv_ref,
    out_hbm, gup_ref, gdn_ref, dep_ref,
    latv, cotv, wu, wd, tt, field, act, hid, slo, dp, dact, turn_g, turn_a, grad, pool, ghost,
    fsend, flow, fupp, k1, s1, r1, s2, r2, s3, u3, r3, r5, r6, dacc, ds1, dr1, dr2, ds3, dr3, ds2,
    in_sem, out_sem, fs_sem, fr_sem, c1s, c1r, c2s, c2r, c3s, c3r, c5s, c5r, c6s, c6r, e_s, e_r,
):
    me_x = lax.axis_index("rep")
    me_p = lax.axis_index("space")
    core = lax.rem(me_p, 2)
    me_q = me_p // 2
    twin = {"rep": me_x, "space": me_p + 1 - 2 * core}
    below = {"rep": me_x, "space": lax.rem(me_p + 31, 32)}
    above = {"rep": me_x, "space": lax.rem(me_p + 1, 32)}

    def along_x(d):
        return {"rep": lax.rem(me_x + d, 4), "space": me_p}

    def along_q(d):
        return {"rep": me_x, "space": lax.rem(me_q + d, 16) * 2 + core}

    loads = [
        pltpu.make_async_copy(a, b, in_sem.at[i])
        for i, (a, b) in enumerate(
            ((lat_hbm, latv), (wu_hbm, wu), (tt_hbm, tt), (wd_hbm, wd), (cot_hbm, cotv))
        )
    ]
    for copy in loads:
        copy.start()

    barrier = pltpu.get_barrier_semaphore()
    for peer in [twin, below, above] + [along_x(d) for d in (1, 2, 3)]:
        pl.semaphore_signal(barrier, inc=1, device_id=peer, device_id_type=MESH)

    @pl.loop(1, 16)
    def _(d):
        pl.semaphore_signal(barrier, inc=1, device_id=along_q(d), device_id_type=MESH)

    def rows_of(s):
        return pl.ds(pl.multiple_of(s * 512, 512), 512)

    def occupied(s):
        return jnp.minimum(jnp.maximum(cnt_ref[0] - s, 0), 1).astype(F32)

    def remote(src, dst, send, recv, peer):
        return pltpu.make_async_remote_copy(
            src_ref=src, dst_ref=dst, send_sem=send, recv_sem=recv, device_id=peer, device_id_type=MESH
        )

    def pool_faces(src):
        @pl.loop(0, 4)
        def _(s):
            for x in range(8):
                plane = src[pl.ds(pl.multiple_of(s * 512 + x * 64, 64), 64), :].astype(F32)
                if x == 0:
                    pool[1 + 4 * s] = plane
                if x == 7:
                    pool[2 + 4 * s] = plane
                pool[3 + 4 * s, x * 8:x * 8 + 8] = plane[:8]
                pool[4 + 4 * s, x * 8:x * 8 + 8] = plane[56:]

    def face_copies(turn):
        return (
            remote(fsend.at[turn, 1], flow.at[turn], fs_sem.at[turn, 1], fr_sem.at[turn, 1], above),
            remote(fsend.at[turn, 0], fupp.at[turn], fs_sem.at[turn, 0], fr_sem.at[turn, 0], below),
        )

    def send_faces(turn):
        for k in range(2):
            for e in range(2):
                fsend[turn, k, e] = pool[1 + snd_ref[0, k, e]].astype(BF)
        for copy in face_copies(turn):
            copy.start()

    def take_faces(turn):
        for copy in face_copies(turn):
            copy.wait()
        lower = jnp.where(me_p > 0, 1.0, 0.0).astype(F32)
        upper = jnp.where(me_p < 31, 1.0, 0.0).astype(F32)
        for e in range(2):
            pool[17 + e] = flow[turn, e].astype(F32) * lower
            pool[19 + e] = fupp[turn, e].astype(F32) * upper

        @pl.loop(0, 4)
        def _(s):
            for side in range(4):
                ghost[s, side] = pool[rcv_ref[s, side]]

    zed = lax.broadcasted_iota(jnp.int32, (8, 128), 0)

    def taps(src, s, cols):
        def plane(x):
            rows = pl.ds(pl.multiple_of(s * 512 + x * 64, 64), 64)
            return src[rows, cols].astype(F32).reshape(8, 8, 128)

        before = ghost[s, 0, :, cols].reshape(8, 8, 128)
        here = plane(0)
        for x in range(8):
            after = plane(x + 1) if x < 7 else ghost[s, 1, :, cols].reshape(8, 8, 128)
            y_low = jnp.concatenate([ghost[s, 2, x * 8:x * 8 + 8, cols][None], here[:7]], axis=0)
            y_upp = jnp.concatenate([here[1:], ghost[s, 3, x * 8:x * 8 + 8, cols][None]], axis=0)
            z_low = pltpu.roll(here, 1, 1)
            z_upp = pltpu.roll(here, 7, 1)
            yield x, (here, before, after, y_low, y_upp, z_low, z_upp)
            before, here = here, after

    def tap_weights(b, cols, order):
        w = [jnp.broadcast_to(dw_ref[b, i:i + 1, cols], (8, 128)) for i in range(7)]
        if order:
            w[5] = jnp.where(zed == 0, 0.0, w[5])
            w[6] = jnp.where(zed == 7, 0.0, w[6])
        else:
            w[5] = jnp.where(zed == 7, 0.0, w[5])
            w[6] = jnp.where(zed == 0, 0.0, w[6])
        return w

    def conv_forward(b):
        for lane in range(2):
            cols = slice(lane * 128, lane * 128 + 128)
            w = tap_weights(b, cols, True)
            shift = jnp.broadcast_to(moment[:, cols], (8, 128))

            @pl.loop(0, 4)
            def _(s):
                for x, near in taps(field.at[b], s, cols):
                    total = shift[None]
                    for i in range(7):
                        total = total + w[i][None] * near[i]
                    rows = pl.ds(pl.multiple_of(s * 512 + x * 64, 64), 64)
                    act[b, rows, cols] = total.reshape(64, 128).astype(BF)

    mirror = (0, 2, 1, 4, 3, 6, 5)

    def conv_backward(b):
        for lane in range(2):
            cols = slice(lane * 128, lane * 128 + 128)
            w = tap_weights(b, cols, False)

            def slot(s, sums):
                occ = occupied(s)
                sums = list(sums)
                for x, near in taps(dact, s, cols):
                    rows = pl.ds(pl.multiple_of(s * 512 + x * 64, 64), 64)
                    total = grad[rows, cols].astype(F32).reshape(8, 8, 128)
                    value = field[b, rows, cols].astype(F32).reshape(8, 8, 128)
                    for i in range(7):
                        total = total + w[i][None] * near[mirror[i]]
                        sums[i] = sums[i] + jnp.sum(value * near[mirror[i]], axis=0)
                    grad[rows, cols] = (total * occ).reshape(64, 128).astype(BF)
                return tuple(sums)

            sums = list(lax.fori_loop(0, 4, slot, tuple(jnp.zeros((8, 128), F32) for _ in range(7))))
            sums[5] = jnp.where(zed == 7, 0.0, sums[5])
            sums[6] = jnp.where(zed == 0, 0.0, sums[6])
            for i in range(7):
                dacc[7 * b + i:7 * b + i + 1, cols] = jnp.sum(sums[i], axis=0, keepdims=True)

    def c1(b, kind):
        return remote(s1.at[b, kind], r1.at[b, kind], c1s.at[b, kind], c1r.at[b, kind], twin)

    def weight_grad(b, kind, left, right):
        @pl.loop(0, 4)
        def _(j):
            tile = dot(left[...], right[:, pl.ds(pl.multiple_of(j * 256, 256), 256)])
            k1[b, kind, j] = tile.reshape(2, 128, 256)
            s1[b, kind, j] = k1[b, kind, j, 1 - core].astype(BF)

        c1(b, kind).start()

    def c2(b, kind, d):
        to = lax.rem(me_x + d, 4)
        return remote(s2.at[b, kind, to], r2.at[b, kind, d - 1], c2s.at[b, kind, d - 1], c2r.at[b, kind, d - 1], along_x(d))

    def step2(b, kind):
        c1(b, kind).wait()
        for d in (2, 1, 3):
            to = lax.rem(me_x + d, 4)
            s2[b, kind, to] = (k1[b, kind, to, core] + r1[b, kind, to].astype(F32)).astype(BF)
            c2(b, kind, d).start()

    def c3(b, d):
        to = lax.rem(me_q + d, 16)
        return remote(s3.at[b, to], r3.at[b, d - 1], c3s.at[b], c3r.at[b], along_q(d))

    def step3(b):
        for kind in range(2):
            for d in (1, 2, 3):
                c2(b, kind, d).wait()
            total = k1[b, kind, me_x, core] + r1[b, kind, me_x].astype(F32)
            for d in range(3):
                total = total + r2[b, kind, d].astype(F32)
            u3[b, kind * 8:kind * 8 + 8] = total.reshape(8, 16, 256)
            s3[b, kind * 8:kind * 8 + 8] = total.reshape(8, 16, 256).astype(BF)

        @pl.loop(1, 16)
        def _(d):
            c3(b, d).start()

    def wait_all(ref, send, recv):
        pltpu.make_async_copy(ref, ref, send).wait()
        pltpu.make_async_copy(ref, ref, recv).wait()

    def c5(b, d):
        return remote(r5.at[b, me_q], r5.at[b, me_q], c5s.at[b], c5r.at[b], along_q(d))

    def step5(b):
        wait_all(r3.at[b], c3s.at[b], c3r.at[b])
        total = u3[b, me_q]
        for d in range(15):
            total = total + r3[b, d].astype(F32)
        r5[b, me_q] = total.astype(BF)

        @pl.loop(1, 16)
        def _(d):
            c5(b, d).start()

    def c6(b):
        return remote(r5.at[b], r6.at[b], c6s.at[b], c6r.at[b], twin)

    def step6(b):
        wait_all(r3.at[b], c5s.at[b], c5r.at[b])
        c6(b).start()

    def finish(b):
        c6(b).wait()
        for side, ref in ((core, r5), (1 - core, r6)):
            at = pl.ds(pl.multiple_of(side * 128, 128), 128)
            gup_ref[b, at, :] = ref[b, 8:].reshape(128, 256).astype(F32) * scale
            gdn_ref[b, :, at] = (ref[b, :8].reshape(128, 256).astype(F32) * scale).T

    def e1():
        return remote(ds1, dr1, e_s.at[0], e_r.at[0], twin)

    def e2(d):
        return remote(ds2, dr2.at[d - 1], e_s.at[d], e_r.at[d], along_x(d))

    def e3(d):
        return remote(ds3, dr3.at[d - 1], e_s.at[4], e_r.at[4], along_q(d))

    loads[0].wait()

    @pl.loop(0, 4)
    def _(s):
        field[0, rows_of(s), :] = (latv[rows_of(s), :].astype(F32) * occupied(s)).astype(BF)

    pool[0] = jnp.zeros((64, 256), F32)
    pool_faces(field.at[0])
    pl.semaphore_wait(barrier, 21)
    send_faces(0)
    loads[2].wait()
    table_row = lax.broadcasted_iota(jnp.int32, (1000, 256), 0)
    moment = jnp.sum(jnp.where(table_row == ts_ref[0], tt[...], 0.0), axis=0, keepdims=True)
    take_faces(0)
    conv_forward(0)
    loads[1].wait()
    loads[3].wait()

    @pl.loop(0, 4)
    def _(s):
        rows = rows_of(s)
        value = act[0, rows, :]
        total = field[0, rows, :].astype(F32)
        for n in range(4):
            part = slice(n * 256, n * 256 + 256)
            hidden, slope = gelu_pair(dot(value, wu[0, :, part]))
            hidden = hidden.astype(BF)
            hid[0, rows, part] = hidden
            slo[rows, part] = slope.astype(BF)
            total = total + dot(hidden, wd[0, part, :])
        field[1, rows, :] = (total * occupied(s)).astype(BF)

    pool_faces(field.at[1])
    send_faces(1)
    loads[4].wait()

    @pl.loop(0, 4)
    def _(s):
        rows = rows_of(s)
        value = (cotv[rows, :].astype(F32) * occupied(s)).astype(BF)
        grad[rows, :] = value
        turn_g[:, rows] = value.T

    take_faces(1)
    conv_forward(1)

    @pl.loop(0, 4)
    def _(s):
        rows = rows_of(s)
        value = act[1, rows, :]
        turn_a[:, rows] = value.T
        down = grad[rows, :]
        total = jnp.zeros((512, 256), F32)
        for n in range(4):
            part = slice(n * 256, n * 256 + 256)
            hidden, slope = gelu_pair(dot(value, wu[1, :, part]))
            hid[1, rows, part] = hidden.astype(BF)
            back = (dot_nt(down, wd[1, part, :]) * slope).astype(BF)
            dp[rows, part] = back
            total = total + dot_nt(back, wu[1, :, part])
        dact[rows, :] = total.astype(BF)

    pool_faces(dact)
    send_faces(2)
    weight_grad(1, 0, turn_g, hid.at[1])
    weight_grad(1, 1, turn_a, dp)
    take_faces(2)
    step2(1, 0)
    step2(1, 1)
    conv_backward(1)

    @pl.loop(0, 4)
    def _(s):
        rows = rows_of(s)
        turn_g[:, rows] = grad[rows, :].T
        turn_a[:, rows] = act[0, rows, :].T

    weight_grad(0, 0, turn_g, hid.at[0])
    step3(1)

    @pl.loop(0, 4)
    def _(s):
        rows = rows_of(s)
        down = grad[rows, :]
        total = jnp.zeros((512, 256), F32)
        for n in range(4):
            part = slice(n * 256, n * 256 + 256)
            back = (dot_nt(down, wd[0, part, :]) * slo[rows, part].astype(F32)).astype(BF)
            dp[rows, part] = back
            total = total + dot_nt(back, wu[0, :, part])
        dact[rows, :] = total.astype(BF)

    pool_faces(dact)
    send_faces(3)
    step2(0, 0)
    weight_grad(0, 1, turn_a, dp)
    step5(1)
    take_faces(3)
    step2(0, 1)
    dacc[14:16] = jnp.zeros((2, 256), F32)
    conv_backward(0)
    out = pltpu.make_async_copy(grad, out_hbm, out_sem)
    out.start()
    ds1[...] = dacc[...].astype(BF)
    e1().start()
    step6(1)
    e1().wait()
    dsum = dacc[...] + dr1[...].astype(F32)
    ds2[...] = dsum.astype(BF)
    for d in (1, 2, 3):
        e2(d).start()
    step3(0)
    for d in (1, 2, 3):
        e2(d).wait()
    for d in range(3):
        dsum = dsum + dr2[d].astype(F32)
    ds3[...] = dsum.astype(BF)

    @pl.loop(1, 16)
    def _(d):
        e3(d).start()

    finish(1)
    step5(0)
    wait_all(dr3, e_s.at[4], e_r.at[4])
    for d in range(15):
        dsum = dsum + dr3[d].astype(F32)
    dsum = dsum * scale
    share = jnp.zeros((16, 64), F32)
    for j in range(4):
        share = jnp.where(me_x == j, dsum[:, j * 64:j * 64 + 64], share)
    dep_ref[0] = share[0:7]
    dep_ref[1] = share[7:14]
    step6(0)
    finish(0)
    out.wait()


def on_device(latents, cotangent, w_up, w_down, depth_w, time_table, timesteps, brick_counts, send_list, recv_list):
    bricks, voxels, channels = latents.shape
    rows = bricks * voxels
    scale = 1.0 / math.sqrt(rows * lax.axis_size("rep") * lax.axis_size("space"))
    anywhere = pl.BlockSpec(memory_space=pl.ANY)
    vmem = pl.BlockSpec(memory_space=pltpu.VMEM)
    smem = pl.BlockSpec(memory_space=pltpu.SMEM)
    dma = pltpu.SemaphoreType.DMA
    out, up, down, depth = pl.pallas_call(
        functools.partial(kernel, scale),
        out_shape=(
            jax.ShapeDtypeStruct((rows, channels), BF),
            jax.ShapeDtypeStruct((2, 256, 256), F32),
            jax.ShapeDtypeStruct((2, 256, 256), F32),
            jax.ShapeDtypeStruct((2, 7, 64), F32),
        ),
        in_specs=[anywhere] * 4 + [vmem, anywhere] + [smem] * 4,
        out_specs=(anywhere, vmem, vmem, vmem),
        scratch_shapes=[
            pltpu.VMEM((rows, 256), BF),
            pltpu.VMEM((rows, 256), BF),
            pltpu.VMEM((2, 256, 1024), BF),
            pltpu.VMEM((2, 1024, 256), BF),
            pltpu.VMEM((1000, 256), F32),
            pltpu.VMEM((2, rows, 256), BF),
            pltpu.VMEM((2, rows, 256), BF),
            pltpu.VMEM((2, rows, 1024), BF),
            pltpu.VMEM((rows, 1024), BF),
            pltpu.VMEM((rows, 1024), BF),
            pltpu.VMEM((rows, 256), BF),
            pltpu.VMEM((256, rows), BF),
            pltpu.VMEM((256, rows), BF),
            pltpu.VMEM((rows, 256), BF),
            pltpu.VMEM((21, 64, 256), F32),
            pltpu.VMEM((4, 4, 64, 256), F32),
            pltpu.VMEM((4, 2, 2, 64, 256), BF),
            pltpu.VMEM((4, 2, 64, 256), BF),
            pltpu.VMEM((4, 2, 64, 256), BF),
            pltpu.VMEM((2, 2, 4, 2, 128, 256), F32),
            pltpu.VMEM((2, 2, 4, 128, 256), BF),
            pltpu.VMEM((2, 2, 4, 128, 256), BF),
            pltpu.VMEM((2, 2, 4, 128, 256), BF),
            pltpu.VMEM((2, 2, 3, 128, 256), BF),
            pltpu.VMEM((2, 16, 16, 256), BF),
            pltpu.VMEM((2, 16, 16, 256), F32),
            pltpu.VMEM((2, 15, 16, 256), BF),
            pltpu.VMEM((2, 16, 16, 256), BF),
            pltpu.VMEM((2, 16, 16, 256), BF),
            pltpu.VMEM((16, 256), F32),
            pltpu.VMEM((16, 256), BF),
            pltpu.VMEM((16, 256), BF),
            pltpu.VMEM((3, 16, 256), BF),
            pltpu.VMEM((16, 256), BF),
            pltpu.VMEM((15, 16, 256), BF),
            pltpu.VMEM((16, 256), BF),
            dma((5,)),
            dma,
            dma((4, 2)),
            dma((4, 2)),
            dma((2, 2)),
            dma((2, 2)),
            dma((2, 2, 3)),
            dma((2, 2, 3)),
            dma((2,)),
            dma((2,)),
            dma((2,)),
            dma((2,)),
            dma((2,)),
            dma((2,)),
            dma((5,)),
            dma((5,)),
        ],
        compiler_params=pltpu.CompilerParams(
            collective_id=0, has_side_effects=True, vmem_limit_bytes=58 * 1024 * 1024
        ),
        name="blocks",
    )(
        latents.reshape(rows, channels),
        cotangent.reshape(rows, channels),
        w_up, w_down, depth_w, time_table, timesteps, brick_counts, send_list, recv_list,
    )
    return out.reshape(latents.shape), up, down, depth


def solution(mesh):
    spread = ("rep", "space")
    return jax.shard_map(
        on_device,
        mesh=mesh,
        in_specs=(
            P(spread, None, None),
            P(spread, None, None),
            P(), P(), P(), P(),
            P("rep"),
            P(spread),
            P(spread, None, None),
            P(spread, None),
        ),
        out_specs=(
            P(spread, None, None),
            P(None, None, "rep"),
            P(None, "rep", None),
            P(None, None, "rep"),
        ),
        check_vma=False,
    )
```

time: 314 us -> 80.8 us (0.26)
  waiting for transfers between devices: 111 us -> 0 us
  Pallas kernels: 0 us -> 71.5 us
  blocking collectives: 65.2 us -> 0 us
  matrix products: 45.3 us -> 0 us
  other arithmetic: 31 us -> 0 us
  starting transfers between devices: 21.2 us -> 0 us
  local copies, waits for them, and re-layouts: 22.7 us -> 6.95 us
  between operations: 16.4 us -> 1.94 us
    psum x1 -> x0, waiting for transfers between devices: 99.6 us -> none  [on_device(): lax.psum(local_up.astype(jnp.bfloat16), 'space').astype(jnp.float32)]
    pallas_call x0 -> x1, Pallas kernels: none -> 71.5 us  [on_device(): pl.pallas_call(functools.partial(kernel, scale), out_shape=(jax.ShapeDtyp...]
    psum x1 -> x0, blocking collectives: 65.2 us -> none  [on_device(): lax.psum(local_depth.astype(jnp.bfloat16), 'space').astype(jnp.float32)]
    dot_general x11 -> x0, matrix products: 45.3 us -> none  [the longest x2 11.8 us: on_device(): lax.dot_general(flat_grad, w_down[block], contract_cols, preferred_elemen...]
    ppermute x8 -> x0, starting transfers between devices: 21.1 us -> none  [from_behind(): lax.ppermute(value, axis, [(source, source + steps) for source in range(i...]
    convert_element_type x14 -> x0, other arithmetic: 15.9 us -> none  [the longest x4 5.19 us: neighbours(): cube = field.reshape(count, E, E, E, width).astype(jnp.float32)]
    concatenate x8 -> x0, other arithmetic: 9.43 us -> none  [the longest x4 6.28 us: neighbours(): along_x = jnp.concatenate([sides[:, 0:1], cube, sides[:, 1:2]], axis=1)]
    gather x8 -> x0, local copies, waits for them, and re-layouts: 7.83 us -> none  [the longest x4 5.61 us: trade_faces(): face_pool[:, recvs.reshape(-1)].reshape(copies, bricks, 4, E * E, channels)]
  transfers between devices with their start and end apart: 12 -> 0, of which waited for: 4 -> 0; matrix products, arithmetic and copies ran while one was open for 9% -> 0% of each run, Pallas kernels for 0% -> 0%
where the time goes in v1:
time: 80.8 us; the launch traced here: 80.4 us
  Pallas kernels  71.5 us (88%)
  local copies, waits for them, and re-layouts  6.95 us (9%)
  between operations  1.94 us (2%)
    pallas_call x1, Pallas kernels, on_device(): pl.pallas_call(functools.partial(kernel, scale), out_shape=(jax.ShapeDtyp...  71.5 us
    unnamed x11, local copies, waits for them, and re-layouts  6.95 us

profile of v1, /device:TPU:1, one launch (start us, length us, event | category | flops | bytes accessed | tf_op | source)
XLA Modules:
  0.0 80.4 jit_solution(1905155555789216794)
XLA Ops:
  1.9 1.3 %copy.14.dw_ref = f32[2,7,256]{2,1,0:T(8,128)} copy(f32[2,7,256]{2,0,1:T(2,128)} %param.14) | data formatting | bytes 28672 | tf_op args[4]
  3.2 71.5 %blocks.1 = (bf16[2048,256]{1,0:T(8,128)(2,1)}, f32[2,256,256]{2,1,0:T(8,128)}, f32[2,256,256]{2,1,0:T(8,128)}, f32[2,7,64]{2,1,0:T(8,128)}) custom-call(bf16[2048,256]{1,0:T(8,128)(2,1)} %bitcast.4, bf16[2048,256]{1,0:T(8,128)(2,1)} %bitcast.5, bf16[2,256,1024]{2,1,0:T(8,128)(2,1)} %wu_hbm.1, bf16[2,1024,256]{2,1,0:T(8,128)(2,1)} %wd_hbm.1, ...), custom_call_target="tpu_custom_call" | custom-call | tf_op jit(solution)/shard_map/blocks/pallas_call | solution.py:421
  74.8 0.0 copy-start.2
  74.8 0.7 copy-done.2
  75.5 0.6 copy.15
  76.1 0.0 copy-start.1
  76.1 2.3 %copy.21 = bf16[4,512,256]{2,1,0:T(8,128)(2,1)} copy(bf16[4,512,256]{2,1,0:T(8,128)(2,1)} %bitcast.3) | data formatting | bytes 2097152
  78.4 0.0 copy-done.1
  78.4 0.0 copy-start
  78.4 0.8 copy.22
  79.2 0.4 copy-done
  79.6 0.8 copy.23
Async XLA Ops:
  74.8 0.7 copy-start.2
  76.1 2.3 %copy-start.1 = (f32[2,256,256]{2,1,0:T(8,128)S(1)}, f32[2,256,256]{2,1,0:T(8,128)}, u32[]{:S(2)}) copy-start(f32[2,256,256]{2,1,0:T(8,128)} %get-tuple-element.21) | copy-start | bytes 1572868
  78.4 1.2 %copy-start = (f32[2,256,256]{2,1,0:T(8,128)S(1)}, f32[2,256,256]{2,1,0:T(8,128)}, u32[]{:S(2)}) copy-start(f32[2,256,256]{2,1,0:T(8,128)} %get-tuple-element.22) | copy-start | bytes 1572868

commit v2 on v1

--- a/solution.py
+++ b/solution.py
@@ -13,30 +13,28 @@
 F32 = jnp.float32
 CUBIC = 0.044715
 ROOT = math.sqrt(2.0 / math.pi)
-NT = (((1,), (1,)), ((), ()))
+LOG2E = math.log2(math.e)
 
 
 def gelu_pair(u):
     square = u * u
-    gate = 0.5 + 0.5 * jnp.tanh(u * (ROOT + (ROOT * CUBIC) * square))
+    power = u * ((-2.0 * ROOT * LOG2E) + (-2.0 * ROOT * CUBIC * LOG2E) * square)
+    e = jnp.exp2(jnp.minimum(power, 80.0))
+    gate = 1.0 / (1.0 + e)
     hidden = u * gate
-    slope = gate + hidden * (1.0 - gate) * (2.0 * ROOT + (6.0 * ROOT * CUBIC) * square)
+    slope = gate + hidden * (e * gate) * ((2.0 * ROOT) + (6.0 * ROOT * CUBIC) * square)
     return hidden, slope
 
 
 def dot(a, b):
     return jnp.dot(a, b, preferred_element_type=F32)
-
-
-def dot_nt(a, b):
-    return lax.dot_general(a, b, NT, preferred_element_type=F32)
 
 
 def kernel(
     scale,
     lat_hbm, cot_hbm, wu_hbm, wd_hbm, dw_ref, tt_hbm, ts_ref, cnt_ref, snd_ref, rcv_ref,
     out_hbm, gup_ref, gdn_ref, dep_ref,
-    latv, cotv, wu, wd, tt, field, act, hid, slo, dp, dact, turn_g, turn_a, grad, pool, ghost,
+    latv, cotv, wu, wd, tt, field, act, hid, slo, dp, dact, turn_g, turn_a, grad, pool, ghost, base, wut, wdt,
     fsend, flow, fupp, k1, s1, r1, s2, r2, s3, u3, r3, r5, r6, dacc, ds1, dr1, dr2, ds3, dr3, ds2,
     in_sem, out_sem, fs_sem, fr_sem, c1s, c1r, c2s, c2r, c3s, c3r, c5s, c5r, c6s, c6r, e_s, e_r,
 ):
@@ -107,7 +105,7 @@
         for copy in face_copies(turn):
             copy.start()
 
-    def take_faces(turn):
+    def take_faces(turn, kept):
         for copy in face_copies(turn):
             copy.wait()
         lower = jnp.where(me_p > 0, 1.0, 0.0).astype(F32)
@@ -119,7 +117,7 @@
         @pl.loop(0, 4)
         def _(s):
             for side in range(4):
-                ghost[s, side] = pool[rcv_ref[s, side]]
+                ghost[kept, s, side] = pool[rcv_ref[s, side]]
 
     zed = lax.broadcasted_iota(jnp.int32, (8, 128), 0)
 
@@ -128,31 +126,26 @@
             rows = pl.ds(pl.multiple_of(s * 512 + x * 64, 64), 64)
             return src[rows, cols].astype(F32).reshape(8, 8, 128)
 
-        before = ghost[s, 0, :, cols].reshape(8, 8, 128)
+        blank = jnp.zeros((1, 8, 128), F32)
+        before = None
         here = plane(0)
         for x in range(8):
-            after = plane(x + 1) if x < 7 else ghost[s, 1, :, cols].reshape(8, 8, 128)
-            y_low = jnp.concatenate([ghost[s, 2, x * 8:x * 8 + 8, cols][None], here[:7]], axis=0)
-            y_upp = jnp.concatenate([here[1:], ghost[s, 3, x * 8:x * 8 + 8, cols][None]], axis=0)
-            z_low = pltpu.roll(here, 1, 1)
-            z_upp = pltpu.roll(here, 7, 1)
-            yield x, (here, before, after, y_low, y_upp, z_low, z_upp)
+            after = plane(x + 1) if x < 7 else None
+            y_low = jnp.concatenate([blank, here[:7]], axis=0)
+            y_upp = jnp.concatenate([here[1:], blank], axis=0)
+            yield x, (here, before, after, y_low, y_upp, pltpu.roll(here, 1, 1), pltpu.roll(here, 7, 1))
             before, here = here, after
 
-    def tap_weights(b, cols, order):
-        w = [jnp.broadcast_to(dw_ref[b, i:i + 1, cols], (8, 128)) for i in range(7)]
-        if order:
-            w[5] = jnp.where(zed == 0, 0.0, w[5])
-            w[6] = jnp.where(zed == 7, 0.0, w[6])
-        else:
-            w[5] = jnp.where(zed == 7, 0.0, w[5])
-            w[6] = jnp.where(zed == 0, 0.0, w[6])
+    def tap_weights(b, cols, low, upp):
+        w = [jnp.broadcast_to(dw_ref[i, b:b + 1, cols], (8, 128)) for i in range(7)]
+        w[5] = jnp.where(zed == low, 0.0, w[5])
+        w[6] = jnp.where(zed == upp, 0.0, w[6])
         return w
 
-    def conv_forward(b):
+    def base_forward(b):
         for lane in range(2):
             cols = slice(lane * 128, lane * 128 + 128)
-            w = tap_weights(b, cols, True)
+            w = tap_weights(b, cols, 0, 7)
             shift = jnp.broadcast_to(moment[:, cols], (8, 128))
 
             @pl.loop(0, 4)
@@ -160,28 +153,56 @@
                 for x, near in taps(field.at[b], s, cols):
                     total = shift[None]
                     for i in range(7):
-                        total = total + w[i][None] * near[i]
+                        if near[i] is not None:
+                            total = total + w[i][None] * near[i]
                     rows = pl.ds(pl.multiple_of(s * 512 + x * 64, 64), 64)
-                    act[b, rows, cols] = total.reshape(64, 128).astype(BF)
+                    base[rows, cols] = total.reshape(64, 128)
+
+    def with_ghosts(kept, s, x, w):
+        total = base[pl.ds(pl.multiple_of(s * 512 + x * 64, 64), 64), :]
+        if x == 0:
+            total = total + w[0] * ghost[kept, s, 0]
+        if x == 7:
+            total = total + w[1] * ghost[kept, s, 1]
+        edge = slice(x * 8, x * 8 + 8)
+        low = total[:8] + w[2] * ghost[kept, s, 2, edge]
+        upp = total[56:] + w[3] * ghost[kept, s, 3, edge]
+        return jnp.concatenate([low, total[8:56], upp], axis=0)
+
+    def finish_forward(b):
+        w = [dw_ref[i, b:b + 1, :] for i in (1, 2, 3, 4)]
+
+        @pl.loop(0, 4)
+        def _(s):
+            for x in range(8):
+                rows = pl.ds(pl.multiple_of(s * 512 + x * 64, 64), 64)
+                act[b, rows, :] = with_ghosts(b, s, x, w).astype(BF)
 
     mirror = (0, 2, 1, 4, 3, 6, 5)
 
-    def conv_backward(b):
+    def base_backward(b):
         for lane in range(2):
             cols = slice(lane * 128, lane * 128 + 128)
-            w = tap_weights(b, cols, False)
+            w = tap_weights(b, cols, 7, 0)
 
             def slot(s, sums):
-                occ = occupied(s)
                 sums = list(sums)
                 for x, near in taps(dact, s, cols):
                     rows = pl.ds(pl.multiple_of(s * 512 + x * 64, 64), 64)
                     total = grad[rows, cols].astype(F32).reshape(8, 8, 128)
                     value = field[b, rows, cols].astype(F32).reshape(8, 8, 128)
+                    here = near[0]
                     for i in range(7):
-                        total = total + w[i][None] * near[mirror[i]]
-                        sums[i] = sums[i] + jnp.sum(value * near[mirror[i]], axis=0)
-                    grad[rows, cols] = (total * occ).reshape(64, 128).astype(BF)
+                        if near[mirror[i]] is not None:
+                            total = total + w[i][None] * near[mirror[i]]
+                            sums[i] = sums[i] + jnp.sum(value * near[mirror[i]], axis=0)
+                    if x == 0:
+                        sums[1] = sums[1] + jnp.sum(ghost[b, s, 0, :, cols].reshape(8, 8, 128) * here, axis=0)
+                    if x == 7:
+                        sums[2] = sums[2] + jnp.sum(ghost[b, s, 1, :, cols].reshape(8, 8, 128) * here, axis=0)
+                    sums[3] = sums[3] + ghost[b, s, 2, x * 8:x * 8 + 8, cols] * here[0]
+                    sums[4] = sums[4] + ghost[b, s, 3, x * 8:x * 8 + 8, cols] * here[7]
+                    base[rows, cols] = total.reshape(64, 128)
                 return tuple(sums)
 
             sums = list(lax.fori_loop(0, 4, slot, tuple(jnp.zeros((8, 128), F32) for _ in range(7))))
@@ -190,16 +211,24 @@
             for i in range(7):
                 dacc[7 * b + i:7 * b + i + 1, cols] = jnp.sum(sums[i], axis=0, keepdims=True)
 
+    def finish_backward(b):
+        w = [dw_ref[i, b:b + 1, :] for i in (2, 1, 4, 3)]
+
+        @pl.loop(0, 4)
+        def _(s):
+            occ = occupied(s)
+            for x in range(8):
+                rows = pl.ds(pl.multiple_of(s * 512 + x * 64, 64), 64)
+                grad[rows, :] = (with_ghosts(2, s, x, w) * occ).astype(BF)
+
     def c1(b, kind):
         return remote(s1.at[b, kind], r1.at[b, kind], c1s.at[b, kind], c1r.at[b, kind], twin)
 
     def weight_grad(b, kind, left, right):
-        @pl.loop(0, 4)
-        def _(j):
-            tile = dot(left[...], right[:, pl.ds(pl.multiple_of(j * 256, 256), 256)])
-            k1[b, kind, j] = tile.reshape(2, 128, 256)
+        tile = dot(left[...], right[...])
+        for j in range(4):
+            k1[b, kind, j] = tile[:, j * 256:j * 256 + 256].reshape(2, 128, 256)
             s1[b, kind, j] = k1[b, kind, j, 1 - core].astype(BF)
-
         c1(b, kind).start()
 
     def c2(b, kind, d):
@@ -272,6 +301,11 @@
     def e3(d):
         return remote(ds3, dr3.at[d - 1], e_s.at[4], e_r.at[4], along_q(d))
 
+    def turn(dst, src):
+        @pl.loop(0, 4)
+        def _(s):
+            dst[:, rows_of(s)] = src[rows_of(s), :].T
+
     loads[0].wait()
 
     @pl.loop(0, 4)
@@ -285,27 +319,12 @@
     loads[2].wait()
     table_row = lax.broadcasted_iota(jnp.int32, (1000, 256), 0)
     moment = jnp.sum(jnp.where(table_row == ts_ref[0], tt[...], 0.0), axis=0, keepdims=True)
-    take_faces(0)
-    conv_forward(0)
+    base_forward(0)
     loads[1].wait()
     loads[3].wait()
-
-    @pl.loop(0, 4)
-    def _(s):
-        rows = rows_of(s)
-        value = act[0, rows, :]
-        total = field[0, rows, :].astype(F32)
-        for n in range(4):
-            part = slice(n * 256, n * 256 + 256)
-            hidden, slope = gelu_pair(dot(value, wu[0, :, part]))
-            hidden = hidden.astype(BF)
-            hid[0, rows, part] = hidden
-            slo[rows, part] = slope.astype(BF)
-            total = total + dot(hidden, wd[0, part, :])
-        field[1, rows, :] = (total * occupied(s)).astype(BF)
-
-    pool_faces(field.at[1])
-    send_faces(1)
+    for b in range(2):
+        wut[b] = wu[b].T
+        wdt[b] = wd[b].T
     loads[4].wait()
 
     @pl.loop(0, 4)
@@ -315,75 +334,69 @@
         grad[rows, :] = value
         turn_g[:, rows] = value.T
 
-    take_faces(1)
-    conv_forward(1)
-
-    @pl.loop(0, 4)
-    def _(s):
-        rows = rows_of(s)
-        value = act[1, rows, :]
-        turn_a[:, rows] = value.T
-        down = grad[rows, :]
-        total = jnp.zeros((512, 256), F32)
-        for n in range(4):
-            part = slice(n * 256, n * 256 + 256)
-            hidden, slope = gelu_pair(dot(value, wu[1, :, part]))
-            hid[1, rows, part] = hidden.astype(BF)
-            back = (dot_nt(down, wd[1, part, :]) * slope).astype(BF)
-            dp[rows, part] = back
-            total = total + dot_nt(back, wu[1, :, part])
-        dact[rows, :] = total.astype(BF)
-
+    take_faces(0, 0)
+    finish_forward(0)
+    for n in range(4):
+        part = slice(n * 256, n * 256 + 256)
+        hid[0, :, part], slo[:, part] = gelu_pair(dot(act[0], wu[0, :, part]).astype(BF))
+    for s in range(4):
+        rows = slice(s * 512, s * 512 + 512)
+        total = field[0, rows, :].astype(F32) + dot(hid[0, rows, :], wd[0])
+        field[1, rows, :] = (total * occupied(s)).astype(BF)
+    pool_faces(field.at[1])
+    send_faces(1)
+    base_forward(1)
+    for n in range(4):
+        part = slice(n * 256, n * 256 + 256)
+        dp[:, part] = dot(grad[...], wdt[1, :, part]).astype(BF)
+    turn(turn_a.at[0], act.at[0])
+    take_faces(1, 1)
+    finish_forward(1)
+
+    for n in range(4):
+        part = slice(n * 256, n * 256 + 256)
+        hidden, slope = gelu_pair(dot(act[1], wu[1, :, part]).astype(BF))
+        hid[1, :, part] = hidden
+        dp[:, part] = dp[:, part] * slope
+    dact[...] = dot(dp[...], wut[1]).astype(BF)
     pool_faces(dact)
     send_faces(2)
     weight_grad(1, 0, turn_g, hid.at[1])
-    weight_grad(1, 1, turn_a, dp)
-    take_faces(2)
+    turn(turn_a.at[1], act.at[1])
+    weight_grad(1, 1, turn_a.at[1], dp)
+    base_backward(1)
     step2(1, 0)
     step2(1, 1)
-    conv_backward(1)
-
-    @pl.loop(0, 4)
-    def _(s):
-        rows = rows_of(s)
-        turn_g[:, rows] = grad[rows, :].T
-        turn_a[:, rows] = act[0, rows, :].T
-
+    take_faces(2, 2)
+    finish_backward(1)
+
+    turn(turn_g, grad)
     weight_grad(0, 0, turn_g, hid.at[0])
-    step3(1)
-
-    @pl.loop(0, 4)
-    def _(s):
-        rows = rows_of(s)
-        down = grad[rows, :]
-        total = jnp.zeros((512, 256), F32)
-        for n in range(4):
-            part = slice(n * 256, n * 256 + 256)
-            back = (dot_nt(down, wd[0, part, :]) * slo[rows, part].astype(F32)).astype(BF)
-            dp[rows, part] = back
-            total = total + dot_nt(back, wu[0, :, part])
-        dact[rows, :] = total.astype(BF)
-
+    for n in range(4):
+        part = slice(n * 256, n * 256 + 256)
+        dp[:, part] = dot(grad[...], wdt[0, :, part]).astype(BF) * slo[:, part]
+    step2(0, 0)
+    weight_grad(0, 1, turn_a.at[0], dp)
+    dact[...] = dot(dp[...], wut[0]).astype(BF)
     pool_faces(dact)
     send_faces(3)
-    step2(0, 0)
-    weight_grad(0, 1, turn_a, dp)
-    step5(1)
-    take_faces(3)
     step2(0, 1)
+    step3(1)
     dacc[14:16] = jnp.zeros((2, 256), F32)
-    conv_backward(0)
+    base_backward(0)
+    ds1[...] = dacc[...].astype(BF)
+    e1().start()
+    take_faces(3, 2)
+    finish_backward(0)
     out = pltpu.make_async_copy(grad, out_hbm, out_sem)
     out.start()
-    ds1[...] = dacc[...].astype(BF)
-    e1().start()
-    step6(1)
     e1().wait()
     dsum = dacc[...] + dr1[...].astype(F32)
     ds2[...] = dsum.astype(BF)
     for d in (1, 2, 3):
         e2(d).start()
     step3(0)
+    step5(1)
     for d in (1, 2, 3):
         e2(d).wait()
     for d in range(3):
@@ -394,8 +407,8 @@
     def _(d):
         e3(d).start()
 
-    finish(1)
     step5(0)
+    step6(1)
     wait_all(dr3, e_s.at[4], e_r.at[4])
     for d in range(15):
         dsum = dsum + dr3[d].astype(F32)
@@ -403,8 +416,10 @@
     share = jnp.zeros((16, 64), F32)
     for j in range(4):
         share = jnp.where(me_x == j, dsum[:, j * 64:j * 64 + 64], share)
-    dep_ref[0] = share[0:7]
-    dep_ref[1] = share[7:14]
+    for i in range(7):
+        dep_ref[i, 0:1] = share[i:i + 1]
+        dep_ref[i, 1:2] = share[7 + i:8 + i]
+    finish(1)
     step6(0)
     finish(0)
     out.wait()
@@ -424,7 +439,7 @@
             jax.ShapeDtypeStruct((rows, channels), BF),
             jax.ShapeDtypeStruct((2, 256, 256), F32),
             jax.ShapeDtypeStruct((2, 256, 256), F32),
-            jax.ShapeDtypeStruct((2, 7, 64), F32),
+            jax.ShapeDtypeStruct((7, 2, 64), F32),
         ),
         in_specs=[anywhere] * 4 + [vmem, anywhere] + [smem] * 4,
         out_specs=(anywhere, vmem, vmem, vmem),
@@ -441,10 +456,13 @@
             pltpu.VMEM((rows, 1024), BF),
             pltpu.VMEM((rows, 256), BF),
             pltpu.VMEM((256, rows), BF),
-            pltpu.VMEM((256, rows), BF),
+            pltpu.VMEM((2, 256, rows), BF),
             pltpu.VMEM((rows, 256), BF),
             pltpu.VMEM((21, 64, 256), F32),
-            pltpu.VMEM((4, 4, 64, 256), F32),
+            pltpu.VMEM((3, 4, 4, 64, 256), F32),
+            pltpu.VMEM((rows, 256), F32),
+            pltpu.VMEM((2, 1024, 256), BF),
+            pltpu.VMEM((2, 256, 1024), BF),
             pltpu.VMEM((4, 2, 2, 64, 256), BF),
             pltpu.VMEM((4, 2, 64, 256), BF),
             pltpu.VMEM((4, 2, 64, 256), BF),
@@ -489,9 +507,9 @@
     )(
         latents.reshape(rows, channels),
         cotangent.reshape(rows, channels),
-        w_up, w_down, depth_w, time_table, timesteps, brick_counts, send_list, recv_list,
+        w_up, w_down, depth_w.transpose(1, 0, 2), time_table, timesteps, brick_counts, send_list, recv_list,
     )
-    return out.reshape(latents.shape), up, down, depth
+    return out.reshape(latents.shape), up, down, depth.transpose(1, 0, 2)
 
 
 def solution(mesh):

time: 80.8 us -> 69 us (0.85)
  Pallas kernels: 71.5 us -> 61.8 us
  local copies, waits for them, and re-layouts: 6.95 us -> 4.94 us
    pallas_call x1, Pallas kernels: 71.5 us -> 61.8 us  [on_device(): pl.pallas_call(functools.partial(kernel, scale), out_shape=(jax.ShapeDtyp...]
    unnamed x11 -> x10, local copies, waits for them, and re-layouts: 6.95 us -> 4.94 us
where the time goes in v2:
time: 69 us; the launch traced here: 68.7 us
  Pallas kernels  61.8 us (90%)
  local copies, waits for them, and re-layouts  4.94 us (7%)
  between operations  1.95 us (3%)
    pallas_call x1, Pallas kernels, on_device(): pl.pallas_call(functools.partial(kernel, scale), out_shape=(jax.ShapeDtyp...  61.8 us
    unnamed x10, local copies, waits for them, and re-layouts  4.94 us

profile of v2, /device:TPU:1, one launch (start us, length us, event | category | flops | bytes accessed | tf_op | source)
XLA Modules:
  0.0 68.7 jit_solution(17251294943120000168)
XLA Ops:
  1.9 61.8 %blocks.1 = (bf16[2048,256]{1,0:T(8,128)(2,1)}, f32[2,256,256]{2,1,0:T(8,128)}, f32[2,256,256]{2,1,0:T(8,128)}, f32[7,2,64]{2,1,0:T(2,128)}) custom-call(bf16[2048,256]{1,0:T(8,128)(2,1)} %bitcast.5, bf16[2048,256]{1,0:T(8,128)(2,1)} %bitcast.6, bf16[2,256,1024]{2,1,0:T(8,128)(2,1)} %wu_hbm.1, bf16[2,1024,256]{2,1,0:T(8,128)(2,1)} %wd_hbm.1, ...), custom_call_target="tpu_custom_call" | custom-call | tf_op jit(solution)/shard_map/blocks/pallas_call | solution.py:436
  63.8 0.0 copy-start.1
  63.8 2.3 %copy.20 = bf16[4,512,256]{2,1,0:T(8,128)(2,1)} copy(bf16[4,512,256]{2,1,0:T(8,128)(2,1)} %bitcast.7) | data formatting | bytes 2097152
  66.1 0.0 copy-done.1
  66.1 0.0 copy-start
  66.1 0.8 %copy.21 = f32[2,256,256]{2,1,0:T(8,128)} copy(f32[2,256,256]{2,1,0:T(8,128)S(1)} %copy-done.1) | data formatting | bytes 1048576
  66.9 0.4 copy-done
  67.3 0.0 copy-start.2
  67.3 0.8 %copy.22 = f32[2,256,256]{2,1,0:T(8,128)} copy(f32[2,256,256]{2,1,0:T(8,128)S(1)} %copy-done) | data formatting | bytes 1048576
  68.1 0.0 copy-done.2
  68.1 0.6 copy.23
Async XLA Ops:
  63.8 2.3 %copy-start.1 = (f32[2,256,256]{2,1,0:T(8,128)S(1)}, f32[2,256,256]{2,1,0:T(8,128)}, u32[]{:S(2)}) copy-start(f32[2,256,256]{2,1,0:T(8,128)} %get-tuple-element.17) | copy-start | bytes 1572868
  66.1 1.2 %copy-start = (f32[2,256,256]{2,1,0:T(8,128)S(1)}, f32[2,256,256]{2,1,0:T(8,128)}, u32[]{:S(2)}) copy-start(f32[2,256,256]{2,1,0:T(8,128)} %get-tuple-element.18) | copy-start | bytes 1572868
  67.3 0.8 %copy-start.2 = (f32[7,2,64]{2,1,0:T(2,128)S(1)}, f32[7,2,64]{2,1,0:T(2,128)}, u32[]{:S(2)}) copy-start(f32[7,2,64]{2,1,0:T(2,128)} %get-tuple-element.11) | copy-start | bytes 10756

commit v3 on v2

--- a/solution.py
+++ b/solution.py
@@ -33,24 +33,31 @@
 def kernel(
     scale,
     lat_hbm, cot_hbm, wu_hbm, wd_hbm, dw_ref, tt_hbm, ts_ref, cnt_ref, snd_ref, rcv_ref,
-    out_hbm, gup_ref, gdn_ref, dep_ref,
+    out_ref, gup_ref, gdn_ref, dep_ref,
     latv, cotv, wu, wd, tt, field, act, hid, slo, dp, dact, turn_g, turn_a, grad, pool, ghost, base, wut, wdt,
-    fsend, flow, fupp, k1, s1, r1, s2, r2, s3, u3, r3, r5, r6, dacc, ds1, dr1, dr2, ds3, dr3, ds2,
-    in_sem, out_sem, fs_sem, fr_sem, c1s, c1r, c2s, c2r, c3s, c3r, c5s, c5r, c6s, c6r, e_s, e_r,
+    fsend, flow, fupp, k1, s1, r1, s2, r2, r3, r5, dacc, ds1, dr1, ds2, dr2, ds3, dr3,
+    in_sem, fs_sem, fr_sem, c1s, c1r, c2s, c2r, c3s, c3r, c5s, c5r, e_s, e_r,
 ):
     me_x = lax.axis_index("rep")
     me_p = lax.axis_index("space")
     core = lax.rem(me_p, 2)
-    me_q = me_p // 2
     twin = {"rep": me_x, "space": me_p + 1 - 2 * core}
     below = {"rep": me_x, "space": lax.rem(me_p + 31, 32)}
     above = {"rep": me_x, "space": lax.rem(me_p + 1, 32)}
 
-    def along_x(d):
-        return {"rep": lax.rem(me_x + d, 4), "space": me_p}
-
-    def along_q(d):
-        return {"rep": me_x, "space": lax.rem(me_q + d, 16) * 2 + core}
+    me_z = me_p // 8
+    me_y = lax.rem(me_p // 2, 4)
+    me_xy = me_x * 4 + me_y
+
+    def along_xy(d):
+        to = lax.rem(me_xy + d, 16)
+        return {"rep": to // 4, "space": me_z * 8 + lax.rem(to, 4) * 2 + core}
+
+    def along_z(d):
+        return {"rep": me_x, "space": lax.rem(me_p + 8 * d, 32)}
+
+    def along_y(d, side):
+        return {"rep": me_x, "space": me_z * 8 + lax.rem(me_y + d, 4) * 2 + side}
 
     loads = [
         pltpu.make_async_copy(a, b, in_sem.at[i])
@@ -62,12 +69,15 @@
         copy.start()
 
     barrier = pltpu.get_barrier_semaphore()
-    for peer in [twin, below, above] + [along_x(d) for d in (1, 2, 3)]:
+    for peer in [twin, below, above] + [along_z(d) for d in (1, 2, 3)]:
         pl.semaphore_signal(barrier, inc=1, device_id=peer, device_id_type=MESH)
+
+    for d in (1, 2, 3):
+        pl.semaphore_signal(barrier, inc=1, device_id=along_y(d, 1 - core), device_id_type=MESH)
 
     @pl.loop(1, 16)
     def _(d):
-        pl.semaphore_signal(barrier, inc=1, device_id=along_q(d), device_id_type=MESH)
+        pl.semaphore_signal(barrier, inc=1, device_id=along_xy(d), device_id_type=MESH)
 
     def rows_of(s):
         return pl.ds(pl.multiple_of(s * 512, 512), 512)
@@ -231,75 +241,69 @@
             s1[b, kind, j] = k1[b, kind, j, 1 - core].astype(BF)
         c1(b, kind).start()
 
-    def c2(b, kind, d):
-        to = lax.rem(me_x + d, 4)
-        return remote(s2.at[b, kind, to], r2.at[b, kind, d - 1], c2s.at[b, kind, d - 1], c2r.at[b, kind, d - 1], along_x(d))
-
-    def step2(b, kind):
-        c1(b, kind).wait()
-        for d in (2, 1, 3):
-            to = lax.rem(me_x + d, 4)
-            s2[b, kind, to] = (k1[b, kind, to, core] + r1[b, kind, to].astype(F32)).astype(BF)
-            c2(b, kind, d).start()
-
-    def c3(b, d):
-        to = lax.rem(me_q + d, 16)
-        return remote(s3.at[b, to], r3.at[b, d - 1], c3s.at[b], c3r.at[b], along_q(d))
-
-    def step3(b):
-        for kind in range(2):
-            for d in (1, 2, 3):
-                c2(b, kind, d).wait()
-            total = k1[b, kind, me_x, core] + r1[b, kind, me_x].astype(F32)
-            for d in range(3):
-                total = total + r2[b, kind, d].astype(F32)
-            u3[b, kind * 8:kind * 8 + 8] = total.reshape(8, 16, 256)
-            s3[b, kind * 8:kind * 8 + 8] = total.reshape(8, 16, 256).astype(BF)
-
-        @pl.loop(1, 16)
-        def _(d):
-            c3(b, d).start()
-
     def wait_all(ref, send, recv):
         pltpu.make_async_copy(ref, ref, send).wait()
         pltpu.make_async_copy(ref, ref, recv).wait()
 
-    def c5(b, d):
-        return remote(r5.at[b, me_q], r5.at[b, me_q], c5s.at[b], c5r.at[b], along_q(d))
-
-    def step5(b):
-        wait_all(r3.at[b], c3s.at[b], c3r.at[b])
-        total = u3[b, me_q]
-        for d in range(15):
-            total = total + r3[b, d].astype(F32)
-        r5[b, me_q] = total.astype(BF)
+    def c2(b, kind, d):
+        to = lax.rem(me_xy + d, 16)
+        return remote(s2.at[b, kind, to], r2.at[b, kind, d - 1], c2s.at[b, kind], c2r.at[b, kind], along_xy(d))
+
+    def step2(b, kind):
+        c1(b, kind).wait()
+        for j in range(4):
+            total = k1[b, kind, j, core] + r1[b, kind, j].astype(F32)
+            s2[b, kind, 4 * j:4 * j + 4] = total.reshape(4, 32, 256).astype(BF)
 
         @pl.loop(1, 16)
         def _(d):
-            c5(b, d).start()
-
-    def c6(b):
-        return remote(r5.at[b], r6.at[b], c6s.at[b], c6r.at[b], twin)
-
-    def step6(b):
-        wait_all(r3.at[b], c5s.at[b], c5r.at[b])
-        c6(b).start()
+            c2(b, kind, d).start()
+
+    def c3(b, d):
+        return remote(r3.at[b, me_z], r3.at[b, me_z], c3s.at[b, d - 1], c3r.at[b, d - 1], along_z(d))
+
+    def step3(b):
+        for kind in range(2):
+            wait_all(r2.at[b, kind], c2s.at[b, kind], c2r.at[b, kind])
+            rows = pl.ds(pl.multiple_of(me_y * 32, 32), 32)
+            total = k1[b, kind, me_x, core, rows] + r1[b, kind, me_x, rows].astype(F32)
+            for d in range(15):
+                total = total + r2[b, kind, d].astype(F32)
+            r3[b, me_z, kind] = total.astype(BF)
+        for d in (2, 1, 3):
+            c3(b, d).start()
+
+    def c5(b, i):
+        peers = [twin] + [along_y(d, side) for d in (1, 2, 3) for side in (core, 1 - core)]
+        return remote(r5.at[b, core, me_y], r5.at[b, core, me_y], c5s.at[b, i], c5r.at[b, i], peers[i])
+
+    def step5(b):
+        for d in (1, 2, 3):
+            c3(b, d).wait()
+        for kind in range(2):
+            total = r3[b, 0, kind].astype(F32)
+            for z in range(1, 4):
+                total = total + r3[b, z, kind].astype(F32)
+            r5[b, core, me_y, kind] = total.astype(BF)
+        for i in (3, 4, 1, 2, 5, 6, 0):
+            c5(b, i).start()
 
     def finish(b):
-        c6(b).wait()
-        for side, ref in ((core, r5), (1 - core, r6)):
-            at = pl.ds(pl.multiple_of(side * 128, 128), 128)
-            gup_ref[b, at, :] = ref[b, 8:].reshape(128, 256).astype(F32) * scale
-            gdn_ref[b, :, at] = (ref[b, :8].reshape(128, 256).astype(F32) * scale).T
+        for i in range(7):
+            c5(b, i).wait()
+        for side in range(2):
+            at = slice(side * 128, side * 128 + 128)
+            gup_ref[b, at, :] = r5[b, side, :, 1].reshape(128, 256).astype(F32) * scale
+            gdn_ref[b, :, at] = (r5[b, side, :, 0].reshape(128, 256).astype(F32) * scale).T
 
     def e1():
         return remote(ds1, dr1, e_s.at[0], e_r.at[0], twin)
 
     def e2(d):
-        return remote(ds2, dr2.at[d - 1], e_s.at[d], e_r.at[d], along_x(d))
+        return remote(ds2, dr2.at[d - 1], e_s.at[1], e_r.at[1], along_xy(d))
 
     def e3(d):
-        return remote(ds3, dr3.at[d - 1], e_s.at[4], e_r.at[4], along_q(d))
+        return remote(ds3, dr3.at[d - 1], e_s.at[1 + d], e_r.at[1 + d], along_z(d))
 
     def turn(dst, src):
         @pl.loop(0, 4)
@@ -314,7 +318,7 @@
 
     pool[0] = jnp.zeros((64, 256), F32)
     pool_faces(field.at[0])
-    pl.semaphore_wait(barrier, 21)
+    pl.semaphore_wait(barrier, 24)
     send_faces(0)
     loads[2].wait()
     table_row = lax.broadcasted_iota(jnp.int32, (1000, 256), 0)
@@ -378,39 +382,38 @@
     step2(0, 0)
     weight_grad(0, 1, turn_a.at[0], dp)
     dact[...] = dot(dp[...], wut[0]).astype(BF)
+    step2(0, 1)
     pool_faces(dact)
     send_faces(3)
-    step2(0, 1)
     step3(1)
     dacc[14:16] = jnp.zeros((2, 256), F32)
     base_backward(0)
     ds1[...] = dacc[...].astype(BF)
     e1().start()
+    step5(1)
     take_faces(3, 2)
     finish_backward(0)
-    out = pltpu.make_async_copy(grad, out_hbm, out_sem)
-    out.start()
+    out_ref[...] = grad[...]
     e1().wait()
     dsum = dacc[...] + dr1[...].astype(F32)
     ds2[...] = dsum.astype(BF)
-    for d in (1, 2, 3):
+
+    @pl.loop(1, 16)
+    def _(d):
         e2(d).start()
+
     step3(0)
-    step5(1)
-    for d in (1, 2, 3):
-        e2(d).wait()
-    for d in range(3):
+    finish(1)
+    wait_all(dr2, e_s.at[1], e_r.at[1])
+    for d in range(15):
         dsum = dsum + dr2[d].astype(F32)
     ds3[...] = dsum.astype(BF)
-
-    @pl.loop(1, 16)
-    def _(d):
+    for d in (1, 2, 3):
         e3(d).start()
-
     step5(0)
-    step6(1)
-    wait_all(dr3, e_s.at[4], e_r.at[4])
-    for d in range(15):
+    for d in (1, 2, 3):
+        e3(d).wait()
+    for d in range(3):
         dsum = dsum + dr3[d].astype(F32)
     dsum = dsum * scale
     share = jnp.zeros((16, 64), F32)
@@ -419,10 +422,7 @@
     for i in range(7):
         dep_ref[i, 0:1] = share[i:i + 1]
         dep_ref[i, 1:2] = share[7 + i:8 + i]
-    finish(1)
-    step6(0)
     finish(0)
-    out.wait()
 
 
 def on_device(latents, cotangent, w_up, w_down, depth_w, time_table, timesteps, brick_counts, send_list, recv_list):
@@ -436,13 +436,13 @@
     out, up, down, depth = pl.pallas_call(
         functools.partial(kernel, scale),
         out_shape=(
-            jax.ShapeDtypeStruct((rows, channels), BF),
-            jax.ShapeDtypeStruct((2, 256, 256), F32),
-            jax.ShapeDtypeStruct((2, 256, 256), F32),
-            jax.ShapeDtypeStruct((7, 2, 64), F32),
+            pltpu.VMEM((rows, channels), BF),
+            pltpu.VMEM((2, 256, 256), F32),
+            pltpu.VMEM((2, 256, 256), F32),
+            pltpu.VMEM((7, 2, 64), F32),
         ),
         in_specs=[anywhere] * 4 + [vmem, anywhere] + [smem] * 4,
-        out_specs=(anywhere, vmem, vmem, vmem),
+        out_specs=(vmem, vmem, vmem, vmem),
         scratch_shapes=[
             pltpu.VMEM((rows, 256), BF),
             pltpu.VMEM((rows, 256), BF),
@@ -469,34 +469,28 @@
             pltpu.VMEM((2, 2, 4, 2, 128, 256), F32),
             pltpu.VMEM((2, 2, 4, 128, 256), BF),
             pltpu.VMEM((2, 2, 4, 128, 256), BF),
-            pltpu.VMEM((2, 2, 4, 128, 256), BF),
-            pltpu.VMEM((2, 2, 3, 128, 256), BF),
-            pltpu.VMEM((2, 16, 16, 256), BF),
-            pltpu.VMEM((2, 16, 16, 256), F32),
-            pltpu.VMEM((2, 15, 16, 256), BF),
-            pltpu.VMEM((2, 16, 16, 256), BF),
-            pltpu.VMEM((2, 16, 16, 256), BF),
+            pltpu.VMEM((2, 2, 16, 32, 256), BF),
+            pltpu.VMEM((2, 2, 15, 32, 256), BF),
+            pltpu.VMEM((2, 4, 2, 32, 256), BF),
+            pltpu.VMEM((2, 2, 4, 2, 32, 256), BF),
             pltpu.VMEM((16, 256), F32),
             pltpu.VMEM((16, 256), BF),
             pltpu.VMEM((16, 256), BF),
-            pltpu.VMEM((3, 16, 256), BF),
             pltpu.VMEM((16, 256), BF),
             pltpu.VMEM((15, 16, 256), BF),
             pltpu.VMEM((16, 256), BF),
+            pltpu.VMEM((3, 16, 256), BF),
             dma((5,)),
-            dma,
             dma((4, 2)),
             dma((4, 2)),
             dma((2, 2)),
             dma((2, 2)),
-            dma((2, 2, 3)),
-            dma((2, 2, 3)),
-            dma((2,)),
-            dma((2,)),
-            dma((2,)),
-            dma((2,)),
-            dma((2,)),
-            dma((2,)),
+            dma((2, 2)),
+            dma((2, 2)),
+            dma((2, 3)),
+            dma((2, 3)),
+            dma((2, 7)),
+            dma((2, 7)),
             dma((5,)),
             dma((5,)),
         ],

time: 69 us -> 66.7 us (0.967)
  local copies, waits for them, and re-layouts: 4.94 us -> 3.15 us
    unnamed x10 -> x4, local copies, waits for them, and re-layouts: 4.94 us -> 3.15 us
where the time goes in v3:
time: 66.7 us; the launch traced here: 66.5 us
  Pallas kernels  61.4 us (92%)
  local copies, waits for them, and re-layouts  3.15 us (5%)
  between operations  1.93 us (3%)
    pallas_call x1, Pallas kernels, on_device(): pl.pallas_call(functools.partial(kernel, scale), out_shape=(pltpu.VMEM((r...  61.4 us
    unnamed x4, local copies, waits for them, and re-layouts  3.15 us

profile of v3, /device:TPU:1, one launch (start us, length us, event | category | flops | bytes accessed | tf_op | source)
XLA Modules:
  0.0 66.5 jit_solution(7661245400239003844)
XLA Ops:
  1.9 61.4 %blocks.1 = (bf16[2048,256]{1,0:T(8,128)(2,1)S(1)}, f32[2,256,256]{2,1,0:T(8,128)S(1)}, f32[2,256,256]{2,1,0:T(8,128)S(1)}, f32[7,2,64]{2,1,0:T(2,128)S(1)}) custom-call(bf16[2048,256]{1,0:T(8,128)(2,1)} %bitcast.7, bf16[2048,256]{1,0:T(8,128)(2,1)} %bitcast.8, bf16[2,256,1024]{2,1,0:T(8,128)(2,1)} %wu_hbm.1, bf16[2,1024,256]{2,1,0:T(8,128)(2,1)} %wd_hbm.1, ...), custom_call_target="tpu_custom_call" | custom-call | tf_op jit(solution)/shard_map/blocks/pallas_call | solution.py:436
  63.3 1.0 %copy.18 = bf16[4,512,256]{2,1,0:T(8,128)(2,1)} copy(bf16[4,512,256]{2,1,0:T(8,128)(2,1)S(1)} %bitcast.5) | data formatting | bytes 2097152
  64.3 0.6 copy.21
  64.9 0.8 %copy.19 = f32[2,256,256]{2,1,0:T(8,128)} copy(f32[2,256,256]{2,1,0:T(8,128)S(1)} %get-tuple-element.13) | data formatting | bytes 1048576
  65.7 0.8 %copy.20 = f32[2,256,256]{2,1,0:T(8,128)} copy(f32[2,256,256]{2,1,0:T(8,128)S(1)} %get-tuple-element.14) | data formatting | bytes 1048576

commit v4 on v3

--- a/solution.py
+++ b/solution.py
@@ -35,7 +35,7 @@
     lat_hbm, cot_hbm, wu_hbm, wd_hbm, dw_ref, tt_hbm, ts_ref, cnt_ref, snd_ref, rcv_ref,
     out_ref, gup_ref, gdn_ref, dep_ref,
     latv, cotv, wu, wd, tt, field, act, hid, slo, dp, dact, turn_g, turn_a, grad, pool, ghost, base, wut, wdt,
-    fsend, flow, fupp, k1, s1, r1, s2, r2, r3, r5, dacc, ds1, dr1, ds2, dr2, ds3, dr3,
+    fsend, flow, fupp, k1, s1, r1, s2, r2, r3, r5, dacc, dsums, ds, dr1, dr2,
     in_sem, fs_sem, fr_sem, c1s, c1r, c2s, c2r, c3s, c3r, c5s, c5r, e_s, e_r,
 ):
     me_x = lax.axis_index("rep")
@@ -190,38 +190,54 @@
 
     mirror = (0, 2, 1, 4, 3, 6, 5)
 
-    def base_backward(b):
-        for lane in range(2):
-            cols = slice(lane * 128, lane * 128 + 128)
-            w = tap_weights(b, cols, 7, 0)
-
-            def slot(s, sums):
-                sums = list(sums)
-                for x, near in taps(dact, s, cols):
-                    rows = pl.ds(pl.multiple_of(s * 512 + x * 64, 64), 64)
-                    total = grad[rows, cols].astype(F32).reshape(8, 8, 128)
-                    value = field[b, rows, cols].astype(F32).reshape(8, 8, 128)
-                    here = near[0]
-                    for i in range(7):
-                        if near[mirror[i]] is not None:
-                            total = total + w[i][None] * near[mirror[i]]
-                            sums[i] = sums[i] + jnp.sum(value * near[mirror[i]], axis=0)
-                    if x == 0:
-                        sums[1] = sums[1] + jnp.sum(ghost[b, s, 0, :, cols].reshape(8, 8, 128) * here, axis=0)
-                    if x == 7:
-                        sums[2] = sums[2] + jnp.sum(ghost[b, s, 1, :, cols].reshape(8, 8, 128) * here, axis=0)
-                    sums[3] = sums[3] + ghost[b, s, 2, x * 8:x * 8 + 8, cols] * here[0]
-                    sums[4] = sums[4] + ghost[b, s, 3, x * 8:x * 8 + 8, cols] * here[7]
-                    base[rows, cols] = total.reshape(64, 128)
-                return tuple(sums)
-
-            sums = list(lax.fori_loop(0, 4, slot, tuple(jnp.zeros((8, 128), F32) for _ in range(7))))
-            sums[5] = jnp.where(zed == 7, 0.0, sums[5])
-            sums[6] = jnp.where(zed == 0, 0.0, sums[6])
-            for i in range(7):
-                dacc[7 * b + i:7 * b + i + 1, cols] = jnp.sum(sums[i], axis=0, keepdims=True)
-
-    def finish_backward(b):
+    def base_backward(b, products):
+        dsums[...] = jnp.zeros((7, 8, 256), F32)
+
+        @pl.loop(0, 2)
+        def _(h):
+            part = pl.ds(pl.multiple_of(h * 512, 512), 512)
+            for kind, left, right in products:
+                tile = dot(left[...], right[:, part])
+                for j in range(2):
+                    k1[b, kind, 2 * h + j] = tile[:, j * 256:j * 256 + 256].reshape(2, 128, 256)
+                    s1[b, kind, 2 * h + j] = k1[b, kind, 2 * h + j, 1 - core].astype(BF)
+            for lane in range(2):
+                cols = slice(lane * 128, lane * 128 + 128)
+                w = tap_weights(b, cols, 7, 0)
+                sums = [dsums[i, :, cols] for i in range(7)]
+                for t in range(2):
+                    s = 2 * h + t
+                    for x, near in taps(dact, s, cols):
+                        rows = pl.ds(pl.multiple_of(s * 512 + x * 64, 64), 64)
+                        total = grad[rows, cols].astype(F32).reshape(8, 8, 128)
+                        value = field[b, rows, cols].astype(F32).reshape(8, 8, 128)
+                        here = near[0]
+                        for i in range(7):
+                            if near[mirror[i]] is not None:
+                                total = total + w[i][None] * near[mirror[i]]
+                                sums[i] = sums[i] + jnp.sum(value * near[mirror[i]], axis=0)
+                        if x == 0:
+                            sums[1] = sums[1] + jnp.sum(ghost[b, s, 0, :, cols].reshape(8, 8, 128) * here, axis=0)
+                        if x == 7:
+                            sums[2] = sums[2] + jnp.sum(ghost[b, s, 1, :, cols].reshape(8, 8, 128) * here, axis=0)
+                        sums[3] = sums[3] + ghost[b, s, 2, x * 8:x * 8 + 8, cols] * here[0]
+                        sums[4] = sums[4] + ghost[b, s, 3, x * 8:x * 8 + 8, cols] * here[7]
+                        base[rows, cols] = total.reshape(64, 128)
+                for i in range(7):
+                    dsums[i, :, cols] = sums[i]
+
+        for kind, left, right in products:
+            c1(b, kind).start()
+        inside = lax.broadcasted_iota(jnp.int32, (8, 256), 0)
+        for i in range(7):
+            total = dsums[i]
+            if i == 5:
+                total = jnp.where(inside == 7, 0.0, total)
+            if i == 6:
+                total = jnp.where(inside == 0, 0.0, total)
+            dacc[7 * b + i:7 * b + i + 1, :] = jnp.sum(total, axis=0, keepdims=True)
+
+    def finish_backward(b, dst):
         w = [dw_ref[i, b:b + 1, :] for i in (2, 1, 4, 3)]
 
         @pl.loop(0, 4)
@@ -229,7 +245,7 @@
             occ = occupied(s)
             for x in range(8):
                 rows = pl.ds(pl.multiple_of(s * 512 + x * 64, 64), 64)
-                grad[rows, :] = (with_ghosts(2, s, x, w) * occ).astype(BF)
+                dst[rows, :] = (with_ghosts(2, s, x, w) * occ).astype(BF)
 
     def c1(b, kind):
         return remote(s1.at[b, kind], r1.at[b, kind], c1s.at[b, kind], c1r.at[b, kind], twin)
@@ -297,18 +313,26 @@
             gdn_ref[b, :, at] = (r5[b, side, :, 0].reshape(128, 256).astype(F32) * scale).T
 
     def e1():
-        return remote(ds1, dr1, e_s.at[0], e_r.at[0], twin)
+        return remote(ds.at[0], dr1, e_s.at[0], e_r.at[0], twin)
 
     def e2(d):
-        return remote(ds2, dr2.at[d - 1], e_s.at[1], e_r.at[1], along_xy(d))
+        return remote(ds.at[1], dr2.at[0, d - 1], e_s.at[d], e_r.at[d], along_xy(4 * d))
 
     def e3(d):
-        return remote(ds3, dr3.at[d - 1], e_s.at[1 + d], e_r.at[1 + d], along_z(d))
-
-    def turn(dst, src):
-        @pl.loop(0, 4)
-        def _(s):
-            dst[:, rows_of(s)] = src[rows_of(s), :].T
+        return remote(ds.at[2], dr2.at[1, d - 1], e_s.at[3 + d], e_r.at[3 + d], along_z(d))
+
+    def e4(d):
+        return remote(ds.at[3], dr2.at[2, d - 1], e_s.at[6 + d], e_r.at[6 + d], along_y(d, core))
+
+    def taps_start(stage, copy):
+        ds[stage] = dacc[...].astype(BF)
+        for d in (2, 1, 3):
+            copy(d).start()
+
+    def taps_take(stage, copy):
+        for d in (1, 2, 3):
+            copy(d).wait()
+        dacc[...] = dacc[...] + dr2[stage - 1, 0].astype(F32) + dr2[stage - 1, 1].astype(F32) + dr2[stage - 1, 2].astype(F32)
 
     loads[0].wait()
 
@@ -353,10 +377,11 @@
     for n in range(4):
         part = slice(n * 256, n * 256 + 256)
         dp[:, part] = dot(grad[...], wdt[1, :, part]).astype(BF)
-    turn(turn_a.at[0], act.at[0])
+    turn_a[0] = act[0].T
     take_faces(1, 1)
     finish_forward(1)
 
+    turn_a[1] = act[1].T
     for n in range(4):
         part = slice(n * 256, n * 256 + 256)
         hidden, slope = gelu_pair(dot(act[1], wu[1, :, part]).astype(BF))
@@ -365,16 +390,13 @@
     dact[...] = dot(dp[...], wut[1]).astype(BF)
     pool_faces(dact)
     send_faces(2)
-    weight_grad(1, 0, turn_g, hid.at[1])
-    turn(turn_a.at[1], act.at[1])
-    weight_grad(1, 1, turn_a.at[1], dp)
-    base_backward(1)
+    base_backward(1, ((0, turn_g, hid.at[1]), (1, turn_a.at[1], dp)))
+    take_faces(2, 2)
+    finish_backward(1, grad)
     step2(1, 0)
     step2(1, 1)
-    take_faces(2, 2)
-    finish_backward(1)
-
-    turn(turn_g, grad)
+
+    turn_g[...] = grad[...].T
     weight_grad(0, 0, turn_g, hid.at[0])
     for n in range(4):
         part = slice(n * 256, n * 256 + 256)
@@ -387,35 +409,24 @@
     send_faces(3)
     step3(1)
     dacc[14:16] = jnp.zeros((2, 256), F32)
-    base_backward(0)
-    ds1[...] = dacc[...].astype(BF)
+    base_backward(0, ())
+    ds[0] = dacc[...].astype(BF)
     e1().start()
     step5(1)
+    e1().wait()
+    dacc[...] = dacc[...] + dr1[...].astype(F32)
+    taps_start(1, e2)
     take_faces(3, 2)
-    finish_backward(0)
-    out_ref[...] = grad[...]
-    e1().wait()
-    dsum = dacc[...] + dr1[...].astype(F32)
-    ds2[...] = dsum.astype(BF)
-
-    @pl.loop(1, 16)
-    def _(d):
-        e2(d).start()
-
+    finish_backward(0, out_ref)
     step3(0)
+    taps_take(1, e2)
+    taps_start(2, e3)
     finish(1)
-    wait_all(dr2, e_s.at[1], e_r.at[1])
-    for d in range(15):
-        dsum = dsum + dr2[d].astype(F32)
-    ds3[...] = dsum.astype(BF)
-    for d in (1, 2, 3):
-        e3(d).start()
     step5(0)
-    for d in (1, 2, 3):
-        e3(d).wait()
-    for d in range(3):
-        dsum = dsum + dr3[d].astype(F32)
-    dsum = dsum * scale
+    taps_take(2, e3)
+    taps_start(3, e4)
+    taps_take(3, e4)
+    dsum = dacc[...] * scale
     share = jnp.zeros((16, 64), F32)
     for j in range(4):
         share = jnp.where(me_x == j, dsum[:, j * 64:j * 64 + 64], share)
@@ -423,6 +434,15 @@
         dep_ref[i, 0:1] = share[i:i + 1]
         dep_ref[i, 1:2] = share[7 + i:8 + i]
     finish(0)
+
+
+def store(*refs):
+    sems = refs[8]
+    copies = [pltpu.make_async_copy(refs[i], refs[4 + i], sems.at[i]) for i in range(4)]
+    for copy in copies:
+        copy.start()
+    for copy in copies:
+        copy.wait()
 
 
 def on_device(latents, cotangent, w_up, w_down, depth_w, time_table, timesteps, brick_counts, send_list, recv_list):
@@ -433,7 +453,7 @@
     vmem = pl.BlockSpec(memory_space=pltpu.VMEM)
     smem = pl.BlockSpec(memory_space=pltpu.SMEM)
     dma = pltpu.SemaphoreType.DMA
-    out, up, down, depth = pl.pallas_call(
+    results = pl.pallas_call(
         functools.partial(kernel, scale),
         out_shape=(
             pltpu.VMEM((rows, channels), BF),
@@ -474,12 +494,10 @@
             pltpu.VMEM((2, 4, 2, 32, 256), BF),
             pltpu.VMEM((2, 2, 4, 2, 32, 256), BF),
             pltpu.VMEM((16, 256), F32),
+            pltpu.VMEM((7, 8, 256), F32),
+            pltpu.VMEM((4, 16, 256), BF),
             pltpu.VMEM((16, 256), BF),
-            pltpu.VMEM((16, 256), BF),
-            pltpu.VMEM((16, 256), BF),
-            pltpu.VMEM((15, 16, 256), BF),
-            pltpu.VMEM((16, 256), BF),
-            pltpu.VMEM((3, 16, 256), BF),
+            pltpu.VMEM((3, 3, 16, 256), BF),
             dma((5,)),
             dma((4, 2)),
             dma((4, 2)),
@@ -491,8 +509,8 @@
             dma((2, 3)),
             dma((2, 7)),
             dma((2, 7)),
-            dma((5,)),
-            dma((5,)),
+            dma((10,)),
+            dma((10,)),
         ],
         compiler_params=pltpu.CompilerParams(
             collective_id=0, has_side_effects=True, vmem_limit_bytes=58 * 1024 * 1024
@@ -503,6 +521,14 @@
         cotangent.reshape(rows, channels),
         w_up, w_down, depth_w.transpose(1, 0, 2), time_table, timesteps, brick_counts, send_list, recv_list,
     )
+    out, up, down, depth = pl.pallas_call(
+        store,
+        out_shape=[jax.ShapeDtypeStruct(a.shape, a.dtype) for a in results],
+        in_specs=[vmem] * 4,
+        out_specs=[anywhere] * 4,
+        scratch_shapes=[dma((4,))],
+        name="store",
+    )(*[pltpu.with_memory_space_constraint(a, pltpu.VMEM) for a in results])
     return out.reshape(latents.shape), up, down, depth.transpose(1, 0, 2)
 
 

time: 66.7 us -> 62.6 us (0.939)
  local copies, waits for them, and re-layouts: 3.15 us -> 0 us
  Pallas kernels: 61.4 us -> 60.3 us
    unnamed x4 -> x0, local copies, waits for them, and re-layouts: 3.15 us -> none
    pallas_call x1, Pallas kernels: 61.4 us -> 58.9 us  [on_device(): pl.pallas_call(functools.partial(kernel, scale), out_shape=(pltpu.VMEM((r...]
    pallas_call x0 -> x1, Pallas kernels: none -> 1.35 us  [on_device(): pl.pallas_call(store, out_shape=[jax.ShapeDtypeStruct(a.shape, a.dtype) f...]
where the time goes in v4:
time: 62.6 us; the launch traced here: 62.3 us
  Pallas kernels  60.3 us (96%)
  between operations  2.09 us (3%)
    pallas_call x1, Pallas kernels, on_device(): pl.pallas_call(functools.partial(kernel, scale), out_shape=(pltpu.VMEM((r...  58.9 us
    pallas_call x1, Pallas kernels, on_device(): pl.pallas_call(store, out_shape=[jax.ShapeDtypeStruct(a.shape, a.dtype) f...  1.35 us

profile of v4, /device:TPU:1, one launch (start us, length us, event | category | flops | bytes accessed | tf_op | source)
XLA Modules:
  0.0 62.3 jit_solution(11979038040494413632)
XLA Ops:
  1.9 58.9 %blocks.1 = (bf16[2048,256]{1,0:T(8,128)(2,1)S(1)}, f32[2,256,256]{2,1,0:T(8,128)S(1)}, f32[2,256,256]{2,1,0:T(8,128)S(1)}, f32[7,2,64]{2,1,0:T(2,128)S(1)}) custom-call(bf16[2048,256]{1,0:T(8,128)(2,1)} %bitcast.5, bf16[2048,256]{1,0:T(8,128)(2,1)} %bitcast.6, bf16[2,256,1024]{2,1,0:T(8,128)(2,1)} %wu_hbm.1, bf16[2,1024,256]{2,1,0:T(8,128)(2,1)} %wd_hbm.1, ...), custom_call_target="tpu_custom_call" | custom-call | tf_op jit(solution)/shard_map/blocks/pallas_call | solution.py:456
  60.8 1.4 %store.1 = (bf16[2048,256]{1,0:T(8,128)(2,1)}, f32[2,256,256]{2,1,0:T(8,128)}, f32[2,256,256]{2,1,0:T(8,128)}, f32[7,2,64]{2,1,0:T(2,128)}) custom-call(bf16[2048,256]{1,0:T(8,128)(2,1)S(1)} %get-tuple-element.12.refs_0_, f32[2,256,256]{2,1,0:T(8,128)S(1)} %get-tuple-element.13.refs_1_, f32[2,256,256]{2,1,0:T(8,128)S(1)} %get-tuple-element.14.refs_2_, ...), custom_call_target="tpu_custom_call" | custom-call | tf_op jit(solution)/shard_map/store/pallas_call | solution.py:524

commit v5 on v4

--- a/solution.py
+++ b/solution.py
@@ -65,19 +65,17 @@
             ((lat_hbm, latv), (wu_hbm, wu), (tt_hbm, tt), (wd_hbm, wd), (cot_hbm, cotv))
         )
     ]
-    for copy in loads:
-        copy.start()
-
+    loads[0].start()
     barrier = pltpu.get_barrier_semaphore()
-    for peer in [twin, below, above] + [along_z(d) for d in (1, 2, 3)]:
-        pl.semaphore_signal(barrier, inc=1, device_id=peer, device_id_type=MESH)
-
-    for d in (1, 2, 3):
-        pl.semaphore_signal(barrier, inc=1, device_id=along_y(d, 1 - core), device_id_type=MESH)
 
     @pl.loop(1, 16)
     def _(d):
         pl.semaphore_signal(barrier, inc=1, device_id=along_xy(d), device_id_type=MESH)
+
+    for peer in [along_z(d) for d in (2, 1, 3)] + [along_y(d, 1 - core) for d in (2, 1, 3)] + [above, below, twin]:
+        pl.semaphore_signal(barrier, inc=1, device_id=peer, device_id_type=MESH)
+    for copy in loads[1:]:
+        copy.start()
 
     def rows_of(s):
         return pl.ds(pl.multiple_of(s * 512, 512), 512)
@@ -101,6 +99,13 @@
                     pool[2 + 4 * s] = plane
                 pool[3 + 4 * s, x * 8:x * 8 + 8] = plane[:8]
                 pool[4 + 4 * s, x * 8:x * 8 + 8] = plane[56:]
+
+    def pool_slot(s, value):
+        planes = value.astype(F32).reshape(8, 64, 256)
+        pool[1 + 4 * s] = planes[0]
+        pool[2 + 4 * s] = planes[7]
+        pool[3 + 4 * s] = planes[:, :8].reshape(64, 256)
+        pool[4 + 4 * s] = planes[:, 56:].reshape(64, 256)
 
     def face_copies(turn):
         return (
@@ -275,42 +280,47 @@
         def _(d):
             c2(b, kind, d).start()
 
-    def c3(b, d):
-        return remote(r3.at[b, me_z], r3.at[b, me_z], c3s.at[b, d - 1], c3r.at[b, d - 1], along_z(d))
-
-    def step3(b):
-        for kind in range(2):
-            wait_all(r2.at[b, kind], c2s.at[b, kind], c2r.at[b, kind])
-            rows = pl.ds(pl.multiple_of(me_y * 32, 32), 32)
-            total = k1[b, kind, me_x, core, rows] + r1[b, kind, me_x, rows].astype(F32)
-            for d in range(15):
-                total = total + r2[b, kind, d].astype(F32)
-            r3[b, me_z, kind] = total.astype(BF)
+    def c3(b, kind, d):
+        return remote(
+            r3.at[b, kind, me_z], r3.at[b, kind, me_z], c3s.at[b, kind, d - 1], c3r.at[b, kind, d - 1], along_z(d)
+        )
+
+    def step3(b, kind):
+        wait_all(r2.at[b, kind], c2s.at[b, kind], c2r.at[b, kind])
+        rows = pl.ds(pl.multiple_of(me_y * 32, 32), 32)
+        total = k1[b, kind, me_x, core, rows] + r1[b, kind, me_x, rows].astype(F32)
+        for d in range(15):
+            total = total + r2[b, kind, d].astype(F32)
+        r3[b, kind, me_z] = total.astype(BF)
         for d in (2, 1, 3):
-            c3(b, d).start()
-
-    def c5(b, i):
+            c3(b, kind, d).start()
+
+    def c5(b, kind, i):
         peers = [twin] + [along_y(d, side) for d in (1, 2, 3) for side in (core, 1 - core)]
-        return remote(r5.at[b, core, me_y], r5.at[b, core, me_y], c5s.at[b, i], c5r.at[b, i], peers[i])
-
-    def step5(b):
+        return remote(
+            r5.at[b, kind, core, me_y], r5.at[b, kind, core, me_y], c5s.at[b, kind, i], c5r.at[b, kind, i], peers[i]
+        )
+
+    def step5(b, kind):
         for d in (1, 2, 3):
-            c3(b, d).wait()
-        for kind in range(2):
-            total = r3[b, 0, kind].astype(F32)
-            for z in range(1, 4):
-                total = total + r3[b, z, kind].astype(F32)
-            r5[b, core, me_y, kind] = total.astype(BF)
+            c3(b, kind, d).wait()
+        total = r3[b, kind, 0].astype(F32)
+        for z in range(1, 4):
+            total = total + r3[b, kind, z].astype(F32)
+        r5[b, kind, core, me_y] = total.astype(BF)
         for i in (3, 4, 1, 2, 5, 6, 0):
-            c5(b, i).start()
-
-    def finish(b):
+            c5(b, kind, i).start()
+
+    def finish(b, kind):
         for i in range(7):
-            c5(b, i).wait()
+            c5(b, kind, i).wait()
         for side in range(2):
             at = slice(side * 128, side * 128 + 128)
-            gup_ref[b, at, :] = r5[b, side, :, 1].reshape(128, 256).astype(F32) * scale
-            gdn_ref[b, :, at] = (r5[b, side, :, 0].reshape(128, 256).astype(F32) * scale).T
+            total = r5[b, kind, side].reshape(128, 256).astype(F32) * scale
+            if kind:
+                gup_ref[b, at, :] = total
+            else:
+                gdn_ref[b, :, at] = total.T
 
     def e1():
         return remote(ds.at[0], dr1, e_s.at[0], e_r.at[0], twin)
@@ -370,8 +380,9 @@
     for s in range(4):
         rows = slice(s * 512, s * 512 + 512)
         total = field[0, rows, :].astype(F32) + dot(hid[0, rows, :], wd[0])
-        field[1, rows, :] = (total * occupied(s)).astype(BF)
-    pool_faces(field.at[1])
+        total = (total * occupied(s)).astype(BF)
+        field[1, rows, :] = total
+        pool_slot(s, total)
     send_faces(1)
     base_forward(1)
     for n in range(4):
@@ -387,13 +398,17 @@
         hidden, slope = gelu_pair(dot(act[1], wu[1, :, part]).astype(BF))
         hid[1, :, part] = hidden
         dp[:, part] = dp[:, part] * slope
-    dact[...] = dot(dp[...], wut[1]).astype(BF)
-    pool_faces(dact)
+    for s in range(4):
+        rows = slice(s * 512, s * 512 + 512)
+        total = dot(dp[rows, :], wut[1]).astype(BF)
+        dact[rows, :] = total
+        pool_slot(s, total)
     send_faces(2)
-    base_backward(1, ((0, turn_g, hid.at[1]), (1, turn_a.at[1], dp)))
+    weight_grad(1, 0, turn_g, hid.at[1])
+    base_backward(1, ((1, turn_a.at[1], dp),))
+    step2(1, 0)
     take_faces(2, 2)
     finish_backward(1, grad)
-    step2(1, 0)
     step2(1, 1)
 
     turn_g[...] = grad[...].T
@@ -403,28 +418,37 @@
         dp[:, part] = dot(grad[...], wdt[0, :, part]).astype(BF) * slo[:, part]
     step2(0, 0)
     weight_grad(0, 1, turn_a.at[0], dp)
-    dact[...] = dot(dp[...], wut[0]).astype(BF)
+    for s in range(4):
+        rows = slice(s * 512, s * 512 + 512)
+        total = dot(dp[rows, :], wut[0]).astype(BF)
+        dact[rows, :] = total
+        pool_slot(s, total)
     step2(0, 1)
-    pool_faces(dact)
     send_faces(3)
-    step3(1)
+    step3(1, 0)
+    step3(1, 1)
     dacc[14:16] = jnp.zeros((2, 256), F32)
     base_backward(0, ())
     ds[0] = dacc[...].astype(BF)
     e1().start()
-    step5(1)
+    step3(0, 0)
     e1().wait()
     dacc[...] = dacc[...] + dr1[...].astype(F32)
     taps_start(1, e2)
     take_faces(3, 2)
     finish_backward(0, out_ref)
-    step3(0)
+    step3(0, 1)
+    step5(1, 0)
+    step5(1, 1)
+    step5(0, 0)
     taps_take(1, e2)
     taps_start(2, e3)
-    finish(1)
-    step5(0)
+    step5(0, 1)
     taps_take(2, e3)
     taps_start(3, e4)
+    finish(1, 0)
+    finish(1, 1)
+    finish(0, 0)
     taps_take(3, e4)
     dsum = dacc[...] * scale
     share = jnp.zeros((16, 64), F32)
@@ -433,7 +457,7 @@
     for i in range(7):
         dep_ref[i, 0:1] = share[i:i + 1]
         dep_ref[i, 1:2] = share[7 + i:8 + i]
-    finish(0)
+    finish(0, 1)
 
 
 def store(*refs):
@@ -491,8 +515,8 @@
             pltpu.VMEM((2, 2, 4, 128, 256), BF),
             pltpu.VMEM((2, 2, 16, 32, 256), BF),
             pltpu.VMEM((2, 2, 15, 32, 256), BF),
-            pltpu.VMEM((2, 4, 2, 32, 256), BF),
-            pltpu.VMEM((2, 2, 4, 2, 32, 256), BF),
+            pltpu.VMEM((2, 2, 4, 32, 256), BF),
+            pltpu.VMEM((2, 2, 2, 4, 32, 256), BF),
             pltpu.VMEM((16, 256), F32),
             pltpu.VMEM((7, 8, 256), F32),
             pltpu.VMEM((4, 16, 256), BF),
@@ -505,10 +529,10 @@
             dma((2, 2)),
             dma((2, 2)),
             dma((2, 2)),
-            dma((2, 3)),
-            dma((2, 3)),
-            dma((2, 7)),
-            dma((2, 7)),
+            dma((2, 2, 3)),
+            dma((2, 2, 3)),
+            dma((2, 2, 7)),
+            dma((2, 2, 7)),
             dma((10,)),
             dma((10,)),
         ],

time: 62.6 us -> 60.2 us (0.962)
  Pallas kernels: 60.3 us -> 57.8 us
    pallas_call x1, Pallas kernels: 58.9 us -> 56.5 us  [on_device(): pl.pallas_call(functools.partial(kernel, scale), out_shape=(pltpu.VMEM((r...]
where the time goes in v5:
time: 60.2 us; the launch traced here: 59.9 us
  Pallas kernels  57.8 us (96%)
  between operations  2.09 us (3%)
    pallas_call x1, Pallas kernels, on_device(): pl.pallas_call(functools.partial(kernel, scale), out_shape=(pltpu.VMEM((r...  56.5 us
    pallas_call x1, Pallas kernels, on_device(): pl.pallas_call(store, out_shape=[jax.ShapeDtypeStruct(a.shape, a.dtype) f...  1.35 us

profile of v5, /device:TPU:1, one launch (start us, length us, event | category | flops | bytes accessed | tf_op | source)
XLA Modules:
  0.0 59.9 jit_solution(4784651873525880421)
XLA Ops:
  1.9 56.5 %blocks.1 = (bf16[2048,256]{1,0:T(8,128)(2,1)S(1)}, f32[2,256,256]{2,1,0:T(8,128)S(1)}, f32[2,256,256]{2,1,0:T(8,128)S(1)}, f32[7,2,64]{2,1,0:T(2,128)S(1)}) custom-call(bf16[2048,256]{1,0:T(8,128)(2,1)} %bitcast.5, bf16[2048,256]{1,0:T(8,128)(2,1)} %bitcast.6, bf16[2,256,1024]{2,1,0:T(8,128)(2,1)} %wu_hbm.1, bf16[2,1024,256]{2,1,0:T(8,128)(2,1)} %wd_hbm.1, ...), custom_call_target="tpu_custom_call" | custom-call | tf_op jit(solution)/shard_map/blocks/pallas_call | solution.py:480
  58.4 1.4 %store.1 = (bf16[2048,256]{1,0:T(8,128)(2,1)}, f32[2,256,256]{2,1,0:T(8,128)}, f32[2,256,256]{2,1,0:T(8,128)}, f32[7,2,64]{2,1,0:T(2,128)}) custom-call(bf16[2048,256]{1,0:T(8,128)(2,1)S(1)} %get-tuple-element.12.refs_0_, f32[2,256,256]{2,1,0:T(8,128)S(1)} %get-tuple-element.13.refs_1_, f32[2,256,256]{2,1,0:T(8,128)S(1)} %get-tuple-element.14.refs_2_, ...), custom_call_target="tpu_custom_call" | custom-call | tf_op jit(solution)/shard_map/store/pallas_call | solution.py:548

commit v6 on v5

--- a/solution.py
+++ b/solution.py
@@ -77,35 +77,51 @@
     for copy in loads[1:]:
         copy.start()
 
-    def rows_of(s):
-        return pl.ds(pl.multiple_of(s * 512, 512), 512)
-
     def occupied(s):
         return jnp.minimum(jnp.maximum(cnt_ref[0] - s, 0), 1).astype(F32)
+
+    def spot(s, x):
+        if x in (0, 7):
+            return pl.ds(pl.multiple_of(s * 224 + (64 if x else 0), 16), 64), None
+        return (
+            pl.ds(pl.multiple_of(s * 224 + 112 + 16 * x, 16), 16),
+            pl.ds(pl.multiple_of(s * 288 + 848 + 48 * x, 16), 48),
+        )
+
+    def load_plane(ref, s, x, cols):
+        edge, inner = spot(s, x)
+        value = ref[edge, cols].astype(F32)
+        width = value.shape[1]
+        if inner is None:
+            return value.reshape(8, 8, width)
+        value = value.reshape(2, 8, width)
+        inside = ref[inner, cols].astype(F32).reshape(6, 8, width)
+        return jnp.concatenate([value[:1], inside, value[1:]], axis=0)
+
+    def store_plane(ref, s, x, value):
+        edge, inner = spot(s, x)
+        value = value.reshape(8, 8, 256)
+        if inner is None:
+            ref[edge, :] = value.reshape(64, 256).astype(BF)
+            return
+        ref[edge, :] = jnp.concatenate([value[:1], value[7:]], axis=0).reshape(16, 256).astype(BF)
+        ref[inner, :] = value[1:7].reshape(48, 256).astype(BF)
+
+    def natural(s, x):
+        return pl.ds(pl.multiple_of(s * 512 + x * 64, 64), 64)
 
     def remote(src, dst, send, recv, peer):
         return pltpu.make_async_remote_copy(
             src_ref=src, dst_ref=dst, send_sem=send, recv_sem=recv, device_id=peer, device_id_type=MESH
         )
 
-    def pool_faces(src):
-        @pl.loop(0, 4)
-        def _(s):
-            for x in range(8):
-                plane = src[pl.ds(pl.multiple_of(s * 512 + x * 64, 64), 64), :].astype(F32)
-                if x == 0:
-                    pool[1 + 4 * s] = plane
-                if x == 7:
-                    pool[2 + 4 * s] = plane
-                pool[3 + 4 * s, x * 8:x * 8 + 8] = plane[:8]
-                pool[4 + 4 * s, x * 8:x * 8 + 8] = plane[56:]
-
-    def pool_slot(s, value):
-        planes = value.astype(F32).reshape(8, 64, 256)
-        pool[1 + 4 * s] = planes[0]
-        pool[2 + 4 * s] = planes[7]
-        pool[3 + 4 * s] = planes[:, :8].reshape(64, 256)
-        pool[4 + 4 * s] = planes[:, 56:].reshape(64, 256)
+    def pool_slot(s, edge):
+        v = edge.astype(F32)
+        middle = [128 + 16 * x for x in range(6)]
+        pool[1 + 4 * s] = v[0:64]
+        pool[2 + 4 * s] = v[64:128]
+        pool[3 + 4 * s] = jnp.concatenate([v[0:8]] + [v[r:r + 8] for r in middle] + [v[64:72]], axis=0)
+        pool[4 + 4 * s] = jnp.concatenate([v[56:64]] + [v[r + 8:r + 16] for r in middle] + [v[120:128]], axis=0)
 
     def face_copies(turn):
         return (
@@ -138,8 +154,7 @@
 
     def taps(src, s, cols):
         def plane(x):
-            rows = pl.ds(pl.multiple_of(s * 512 + x * 64, 64), 64)
-            return src[rows, cols].astype(F32).reshape(8, 8, 128)
+            return load_plane(src, s, x, cols)
 
         blank = jnp.zeros((1, 8, 128), F32)
         before = None
@@ -190,8 +205,7 @@
         @pl.loop(0, 4)
         def _(s):
             for x in range(8):
-                rows = pl.ds(pl.multiple_of(s * 512 + x * 64, 64), 64)
-                act[b, rows, :] = with_ghosts(b, s, x, w).astype(BF)
+                store_plane(act.at[b], s, x, with_ghosts(b, s, x, w))
 
     mirror = (0, 2, 1, 4, 3, 6, 5)
 
@@ -214,8 +228,8 @@
                     s = 2 * h + t
                     for x, near in taps(dact, s, cols):
                         rows = pl.ds(pl.multiple_of(s * 512 + x * 64, 64), 64)
-                        total = grad[rows, cols].astype(F32).reshape(8, 8, 128)
-                        value = field[b, rows, cols].astype(F32).reshape(8, 8, 128)
+                        total = load_plane(grad, s, x, cols)
+                        value = load_plane(field.at[b], s, x, cols)
                         here = near[0]
                         for i in range(7):
                             if near[mirror[i]] is not None:
@@ -242,15 +256,18 @@
                 total = jnp.where(inside == 0, 0.0, total)
             dacc[7 * b + i:7 * b + i + 1, :] = jnp.sum(total, axis=0, keepdims=True)
 
-    def finish_backward(b, dst):
+    def finish_backward(b):
         w = [dw_ref[i, b:b + 1, :] for i in (2, 1, 4, 3)]
 
         @pl.loop(0, 4)
         def _(s):
             occ = occupied(s)
             for x in range(8):
-                rows = pl.ds(pl.multiple_of(s * 512 + x * 64, 64), 64)
-                dst[rows, :] = (with_ghosts(2, s, x, w) * occ).astype(BF)
+                total = with_ghosts(2, s, x, w) * occ
+                if b:
+                    store_plane(grad, s, x, total)
+                else:
+                    out_ref[natural(s, x), :] = total.astype(BF)
 
     def c1(b, kind):
         return remote(s1.at[b, kind], r1.at[b, kind], c1s.at[b, kind], c1r.at[b, kind], twin)
@@ -346,12 +363,21 @@
 
     loads[0].wait()
 
+    pool[0] = jnp.zeros((64, 256), F32)
+
     @pl.loop(0, 4)
     def _(s):
-        field[0, rows_of(s), :] = (latv[rows_of(s), :].astype(F32) * occupied(s)).astype(BF)
-
-    pool[0] = jnp.zeros((64, 256), F32)
-    pool_faces(field.at[0])
+        occ = occupied(s)
+        for x in range(8):
+            plane = latv[natural(s, x), :].astype(F32) * occ
+            store_plane(field.at[0], s, x, plane)
+            if x == 0:
+                pool[1 + 4 * s] = plane
+            if x == 7:
+                pool[2 + 4 * s] = plane
+            pool[3 + 4 * s, x * 8:x * 8 + 8] = plane[:8]
+            pool[4 + 4 * s, x * 8:x * 8 + 8] = plane[56:]
+
     pl.semaphore_wait(barrier, 24)
     send_faces(0)
     loads[2].wait()
@@ -367,23 +393,27 @@
 
     @pl.loop(0, 4)
     def _(s):
-        rows = rows_of(s)
-        value = (cotv[rows, :].astype(F32) * occupied(s)).astype(BF)
-        grad[rows, :] = value
-        turn_g[:, rows] = value.T
-
+        occ = occupied(s)
+        for x in range(8):
+            store_plane(grad, s, x, cotv[natural(s, x), :].astype(F32) * occ)
+
+    turn_g[...] = grad[...].T
     take_faces(0, 0)
     finish_forward(0)
-    for n in range(4):
-        part = slice(n * 256, n * 256 + 256)
-        hid[0, :, part], slo[:, part] = gelu_pair(dot(act[0], wu[0, :, part]).astype(BF))
-    for s in range(4):
-        rows = slice(s * 512, s * 512 + 512)
-        total = field[0, rows, :].astype(F32) + dot(hid[0, rows, :], wd[0])
-        total = (total * occupied(s)).astype(BF)
-        field[1, rows, :] = total
-        pool_slot(s, total)
-    send_faces(1)
+    for first, size in ((0, 224), (896, 288)):
+        group = slice(first, first + 4 * size)
+        for n in range(4):
+            part = slice(n * 256, n * 256 + 256)
+            hid[0, group, part], slo[group, part] = gelu_pair(dot(act[0, group, :], wu[0, :, part]).astype(BF))
+        for s in range(4):
+            rows = slice(first + s * size, first + s * size + size)
+            total = field[0, rows, :].astype(F32) + dot(hid[0, rows, :], wd[0])
+            total = (total * occupied(s)).astype(BF)
+            field[1, rows, :] = total
+            if first == 0:
+                pool_slot(s, total)
+        if first == 0:
+            send_faces(1)
     base_forward(1)
     for n in range(4):
         part = slice(n * 256, n * 256 + 256)
@@ -399,16 +429,17 @@
         hid[1, :, part] = hidden
         dp[:, part] = dp[:, part] * slope
     for s in range(4):
-        rows = slice(s * 512, s * 512 + 512)
+        rows = slice(s * 224, s * 224 + 224)
         total = dot(dp[rows, :], wut[1]).astype(BF)
         dact[rows, :] = total
         pool_slot(s, total)
     send_faces(2)
+    dact[896:, :] = dot(dp[896:, :], wut[1]).astype(BF)
     weight_grad(1, 0, turn_g, hid.at[1])
     base_backward(1, ((1, turn_a.at[1], dp),))
     step2(1, 0)
     take_faces(2, 2)
-    finish_backward(1, grad)
+    finish_backward(1)
     step2(1, 1)
 
     turn_g[...] = grad[...].T
@@ -419,12 +450,13 @@
     step2(0, 0)
     weight_grad(0, 1, turn_a.at[0], dp)
     for s in range(4):
-        rows = slice(s * 512, s * 512 + 512)
+        rows = slice(s * 224, s * 224 + 224)
         total = dot(dp[rows, :], wut[0]).astype(BF)
         dact[rows, :] = total
         pool_slot(s, total)
+    send_faces(3)
+    dact[896:, :] = dot(dp[896:, :], wut[0]).astype(BF)
     step2(0, 1)
-    send_faces(3)
     step3(1, 0)
     step3(1, 1)
     dacc[14:16] = jnp.zeros((2, 256), F32)
@@ -436,7 +468,7 @@
     dacc[...] = dacc[...] + dr1[...].astype(F32)
     taps_start(1, e2)
     take_faces(3, 2)
-    finish_backward(0, out_ref)
+    finish_backward(0)
     step3(0, 1)
     step5(1, 0)
     step5(1, 1)

time: 60.2 us -> 59.2 us (0.983)
  Pallas kernels: 57.8 us -> 56.9 us
    pallas_call x1, Pallas kernels: 56.5 us -> 55.6 us  [on_device(): pl.pallas_call(functools.partial(kernel, scale), out_shape=(pltpu.VMEM((r...]
where the time goes in v6:
time: 59.2 us; the launch traced here: 59 us
  Pallas kernels  56.9 us (96%)
  between operations  2.11 us (4%)
    pallas_call x1, Pallas kernels, on_device(): pl.pallas_call(functools.partial(kernel, scale), out_shape=(pltpu.VMEM((r...  55.6 us
    pallas_call x1, Pallas kernels, on_device(): pl.pallas_call(store, out_shape=[jax.ShapeDtypeStruct(a.shape, a.dtype) f...  1.35 us

profile of v6, /device:TPU:1, one launch (start us, length us, event | category | flops | bytes accessed | tf_op | source)
XLA Modules:
  0.0 59.0 jit_solution(10513426713964738519)
XLA Ops:
  1.9 55.6 %blocks.1 = (bf16[2048,256]{1,0:T(8,128)(2,1)S(1)}, f32[2,256,256]{2,1,0:T(8,128)S(1)}, f32[2,256,256]{2,1,0:T(8,128)S(1)}, f32[7,2,64]{2,1,0:T(2,128)S(1)}) custom-call(bf16[2048,256]{1,0:T(8,128)(2,1)} %bitcast.5, bf16[2048,256]{1,0:T(8,128)(2,1)} %bitcast.6, bf16[2,256,1024]{2,1,0:T(8,128)(2,1)} %wu_hbm.1, bf16[2,1024,256]{2,1,0:T(8,128)(2,1)} %wd_hbm.1, ...), custom_call_target="tpu_custom_call" | custom-call | tf_op jit(solution)/shard_map/blocks/pallas_call | solution.py:512
  57.5 1.4 %store.1 = (bf16[2048,256]{1,0:T(8,128)(2,1)}, f32[2,256,256]{2,1,0:T(8,128)}, f32[2,256,256]{2,1,0:T(8,128)}, f32[7,2,64]{2,1,0:T(2,128)}) custom-call(bf16[2048,256]{1,0:T(8,128)(2,1)S(1)} %get-tuple-element.12.refs_0_, f32[2,256,256]{2,1,0:T(8,128)S(1)} %get-tuple-element.13.refs_1_, f32[2,256,256]{2,1,0:T(8,128)S(1)} %get-tuple-element.14.refs_2_, ...), custom_call_target="tpu_custom_call" | custom-call | tf_op jit(solution)/shard_map/store/pallas_call | solution.py:580

commit v7 on v6

--- a/solution.py
+++ b/solution.py
@@ -136,7 +136,7 @@
         for copy in face_copies(turn):
             copy.start()
 
-    def take_faces(turn, kept):
+    def take_faces(turn):
         for copy in face_copies(turn):
             copy.wait()
         lower = jnp.where(me_p > 0, 1.0, 0.0).astype(F32)
@@ -144,11 +144,6 @@
         for e in range(2):
             pool[17 + e] = flow[turn, e].astype(F32) * lower
             pool[19 + e] = fupp[turn, e].astype(F32) * upper
-
-        @pl.loop(0, 4)
-        def _(s):
-            for side in range(4):
-                ghost[kept, s, side] = pool[rcv_ref[s, side]]
 
     zed = lax.broadcasted_iota(jnp.int32, (8, 128), 0)
 
@@ -188,15 +183,15 @@
                     rows = pl.ds(pl.multiple_of(s * 512 + x * 64, 64), 64)
                     base[rows, cols] = total.reshape(64, 128)
 
-    def with_ghosts(kept, s, x, w):
+    def with_ghosts(sides, s, x, w):
         total = base[pl.ds(pl.multiple_of(s * 512 + x * 64, 64), 64), :]
         if x == 0:
-            total = total + w[0] * ghost[kept, s, 0]
+            total = total + w[0] * sides[0]
         if x == 7:
-            total = total + w[1] * ghost[kept, s, 1]
+            total = total + w[1] * sides[1]
         edge = slice(x * 8, x * 8 + 8)
-        low = total[:8] + w[2] * ghost[kept, s, 2, edge]
-        upp = total[56:] + w[3] * ghost[kept, s, 3, edge]
+        low = total[:8] + w[2] * sides[2][edge]
+        upp = total[56:] + w[3] * sides[3][edge]
         return jnp.concatenate([low, total[8:56], upp], axis=0)
 
     def finish_forward(b):
@@ -204,8 +199,11 @@
 
         @pl.loop(0, 4)
         def _(s):
+            sides = [pool[rcv_ref[s, side]] for side in range(4)]
+            for side in range(4):
+                ghost[b, s, side] = sides[side]
             for x in range(8):
-                store_plane(act.at[b], s, x, with_ghosts(b, s, x, w))
+                store_plane(act.at[b], s, x, with_ghosts(sides, s, x, w))
 
     mirror = (0, 2, 1, 4, 3, 6, 5)
 
@@ -262,8 +260,9 @@
         @pl.loop(0, 4)
         def _(s):
             occ = occupied(s)
+            sides = [pool[rcv_ref[s, side]] for side in range(4)]
             for x in range(8):
-                total = with_ghosts(2, s, x, w) * occ
+                total = with_ghosts(sides, s, x, w) * occ
                 if b:
                     store_plane(grad, s, x, total)
                 else:
@@ -283,9 +282,12 @@
         pltpu.make_async_copy(ref, ref, send).wait()
         pltpu.make_async_copy(ref, ref, recv).wait()
 
-    def c2(b, kind, d):
-        to = lax.rem(me_xy + d, 16)
-        return remote(s2.at[b, kind, to], r2.at[b, kind, d - 1], c2s.at[b, kind], c2r.at[b, kind], along_xy(d))
+    def c2(b, kind, dx, dy):
+        x, y = lax.rem(me_x + dx, 4), lax.rem(me_y + dy, 4)
+        peer = {"rep": x, "space": me_z * 8 + y * 2 + core}
+        return remote(
+            s2.at[b, kind, x * 4 + y], r2.at[b, kind, dx * 4 + dy - 1], c2s.at[b, kind], c2r.at[b, kind], peer
+        )
 
     def step2(b, kind):
         c1(b, kind).wait()
@@ -293,9 +295,10 @@
             total = k1[b, kind, j, core] + r1[b, kind, j].astype(F32)
             s2[b, kind, 4 * j:4 * j + 4] = total.reshape(4, 32, 256).astype(BF)
 
-        @pl.loop(1, 16)
-        def _(d):
-            c2(b, kind, d).start()
+        for dx, dy in ((2, 2), (2, 1), (1, 2), (2, 3), (3, 2), (1, 1), (1, 3), (3, 1), (3, 3)):
+            c2(b, kind, dx, dy).start()
+        for dx, dy in ((2, 0), (0, 2), (1, 0), (0, 1), (3, 0), (0, 3)):
+            c2(b, kind, dx, dy).start()
 
     def c3(b, kind, d):
         return remote(
@@ -398,7 +401,10 @@
             store_plane(grad, s, x, cotv[natural(s, x), :].astype(F32) * occ)
 
     turn_g[...] = grad[...].T
-    take_faces(0, 0)
+    for n in range(4):
+        part = slice(n * 256, n * 256 + 256)
+        dp[:, part] = dot(grad[...], wdt[1, :, part]).astype(BF)
+    take_faces(0)
     finish_forward(0)
     for first, size in ((0, 224), (896, 288)):
         group = slice(first, first + 4 * size)
@@ -415,11 +421,8 @@
         if first == 0:
             send_faces(1)
     base_forward(1)
-    for n in range(4):
-        part = slice(n * 256, n * 256 + 256)
-        dp[:, part] = dot(grad[...], wdt[1, :, part]).astype(BF)
     turn_a[0] = act[0].T
-    take_faces(1, 1)
+    take_faces(1)
     finish_forward(1)
 
     turn_a[1] = act[1].T
@@ -438,7 +441,7 @@
     weight_grad(1, 0, turn_g, hid.at[1])
     base_backward(1, ((1, turn_a.at[1], dp),))
     step2(1, 0)
-    take_faces(2, 2)
+    take_faces(2)
     finish_backward(1)
     step2(1, 1)
 
@@ -467,7 +470,7 @@
     e1().wait()
     dacc[...] = dacc[...] + dr1[...].astype(F32)
     taps_start(1, e2)
-    take_faces(3, 2)
+    take_faces(3)
     finish_backward(0)
     step3(0, 1)
     step5(1, 0)
@@ -535,7 +538,7 @@
             pltpu.VMEM((2, 256, rows), BF),
             pltpu.VMEM((rows, 256), BF),
             pltpu.VMEM((21, 64, 256), F32),
-            pltpu.VMEM((3, 4, 4, 64, 256), F32),
+            pltpu.VMEM((2, 4, 4, 64, 256), F32),
             pltpu.VMEM((rows, 256), F32),
             pltpu.VMEM((2, 1024, 256), BF),
             pltpu.VMEM((2, 256, 1024), BF),

time: 59.2 us -> 57.2 us (0.966)
  Pallas kernels: 56.9 us -> 54.9 us
    pallas_call x1, Pallas kernels: 55.6 us -> 53.5 us  [on_device(): pl.pallas_call(functools.partial(kernel, scale), out_shape=(pltpu.VMEM((r...]
where the time goes in v7:
time: 57.2 us; the launch traced here: 57 us
  Pallas kernels  54.9 us (96%)
  between operations  2.11 us (4%)
    pallas_call x1, Pallas kernels, on_device(): pl.pallas_call(functools.partial(kernel, scale), out_shape=(pltpu.VMEM((r...  53.5 us
    pallas_call x1, Pallas kernels, on_device(): pl.pallas_call(store, out_shape=[jax.ShapeDtypeStruct(a.shape, a.dtype) f...  1.35 us

profile of v7, /device:TPU:1, one launch (start us, length us, event | category | flops | bytes accessed | tf_op | source)
XLA Modules:
  0.0 57.0 jit_solution(1308317700022138565)
XLA Ops:
  1.9 53.5 %blocks.1 = (bf16[2048,256]{1,0:T(8,128)(2,1)S(1)}, f32[2,256,256]{2,1,0:T(8,128)S(1)}, f32[2,256,256]{2,1,0:T(8,128)S(1)}, f32[7,2,64]{2,1,0:T(2,128)S(1)}) custom-call(bf16[2048,256]{1,0:T(8,128)(2,1)} %bitcast.5, bf16[2048,256]{1,0:T(8,128)(2,1)} %bitcast.6, bf16[2,256,1024]{2,1,0:T(8,128)(2,1)} %wu_hbm.1, bf16[2,1024,256]{2,1,0:T(8,128)(2,1)} %wd_hbm.1, ...), custom_call_target="tpu_custom_call" | custom-call | tf_op jit(solution)/shard_map/blocks/pallas_call | solution.py:515
  55.5 1.4 %store.1 = (bf16[2048,256]{1,0:T(8,128)(2,1)}, f32[2,256,256]{2,1,0:T(8,128)}, f32[2,256,256]{2,1,0:T(8,128)}, f32[7,2,64]{2,1,0:T(2,128)}) custom-call(bf16[2048,256]{1,0:T(8,128)(2,1)S(1)} %get-tuple-element.12.refs_0_, f32[2,256,256]{2,1,0:T(8,128)S(1)} %get-tuple-element.13.refs_1_, f32[2,256,256]{2,1,0:T(8,128)S(1)} %get-tuple-element.14.refs_2_, ...), custom_call_target="tpu_custom_call" | custom-call | tf_op jit(solution)/shard_map/store/pallas_call | solution.py:583

commit v8 on v7

--- a/solution.py
+++ b/solution.py
@@ -9,6 +9,9 @@
 from jax.sharding import PartitionSpec as P
 
 MESH = pl.DeviceIdType.MESH
+FAR_FIRST = (
+    (2, 2), (2, 1), (1, 2), (2, 3), (3, 2), (1, 1), (1, 3), (3, 1), (3, 3), (2, 0), (0, 2), (1, 0), (0, 1), (3, 0), (0, 3),
+)
 BF = jnp.bfloat16
 F32 = jnp.float32
 CUBIC = 0.044715
@@ -47,11 +50,9 @@
 
     me_z = me_p // 8
     me_y = lax.rem(me_p // 2, 4)
-    me_xy = me_x * 4 + me_y
-
-    def along_xy(d):
-        to = lax.rem(me_xy + d, 16)
-        return {"rep": to // 4, "space": me_z * 8 + lax.rem(to, 4) * 2 + core}
+
+    def offset_xy(dx, dy):
+        return {"rep": lax.rem(me_x + dx, 4), "space": me_z * 8 + lax.rem(me_y + dy, 4) * 2 + core}
 
     def along_z(d):
         return {"rep": me_x, "space": lax.rem(me_p + 8 * d, 32)}
@@ -68,10 +69,8 @@
     loads[0].start()
     barrier = pltpu.get_barrier_semaphore()
 
-    @pl.loop(1, 16)
-    def _(d):
-        pl.semaphore_signal(barrier, inc=1, device_id=along_xy(d), device_id_type=MESH)
-
+    for dx, dy in FAR_FIRST:
+        pl.semaphore_signal(barrier, inc=1, device_id=offset_xy(dx, dy), device_id_type=MESH)
     for peer in [along_z(d) for d in (2, 1, 3)] + [along_y(d, 1 - core) for d in (2, 1, 3)] + [above, below, twin]:
         pl.semaphore_signal(barrier, inc=1, device_id=peer, device_id_type=MESH)
     for copy in loads[1:]:
@@ -284,9 +283,9 @@
 
     def c2(b, kind, dx, dy):
         x, y = lax.rem(me_x + dx, 4), lax.rem(me_y + dy, 4)
-        peer = {"rep": x, "space": me_z * 8 + y * 2 + core}
         return remote(
-            s2.at[b, kind, x * 4 + y], r2.at[b, kind, dx * 4 + dy - 1], c2s.at[b, kind], c2r.at[b, kind], peer
+            s2.at[b, kind, x * 4 + y], r2.at[b, kind, dx * 4 + dy - 1], c2s.at[b, kind], c2r.at[b, kind],
+            offset_xy(dx, dy),
         )
 
     def step2(b, kind):
@@ -295,9 +294,7 @@
             total = k1[b, kind, j, core] + r1[b, kind, j].astype(F32)
             s2[b, kind, 4 * j:4 * j + 4] = total.reshape(4, 32, 256).astype(BF)
 
-        for dx, dy in ((2, 2), (2, 1), (1, 2), (2, 3), (3, 2), (1, 1), (1, 3), (3, 1), (3, 3)):
-            c2(b, kind, dx, dy).start()
-        for dx, dy in ((2, 0), (0, 2), (1, 0), (0, 1), (3, 0), (0, 3)):
+        for dx, dy in FAR_FIRST:
             c2(b, kind, dx, dy).start()
 
     def c3(b, kind, d):
@@ -346,7 +343,7 @@
         return remote(ds.at[0], dr1, e_s.at[0], e_r.at[0], twin)
 
     def e2(d):
-        return remote(ds.at[1], dr2.at[0, d - 1], e_s.at[d], e_r.at[d], along_xy(4 * d))
+        return remote(ds.at[1], dr2.at[0, d - 1], e_s.at[d], e_r.at[d], offset_xy(d, 0))
 
     def e3(d):
         return remote(ds.at[2], dr2.at[1, d - 1], e_s.at[3 + d], e_r.at[3 + d], along_z(d))

time: 57.2 us -> 56.9 us (level)
  no operation moved by 1% of the time
where the time goes in v8:
time: 56.9 us; the launch traced here: 56.7 us
  Pallas kernels  54.6 us (96%)
  between operations  2.11 us (4%)
    pallas_call x1, Pallas kernels, on_device(): pl.pallas_call(functools.partial(kernel, scale), out_shape=(pltpu.VMEM((r...  53.3 us
    pallas_call x1, Pallas kernels, on_device(): pl.pallas_call(store, out_shape=[jax.ShapeDtypeStruct(a.shape, a.dtype) f...  1.35 us

profile of v8, /device:TPU:1, one launch (start us, length us, event | category | flops | bytes accessed | tf_op | source)
XLA Modules:
  0.0 56.7 jit_solution(18144304407777591444)
XLA Ops:
  1.9 53.3 %blocks.1 = (bf16[2048,256]{1,0:T(8,128)(2,1)S(1)}, f32[2,256,256]{2,1,0:T(8,128)S(1)}, f32[2,256,256]{2,1,0:T(8,128)S(1)}, f32[7,2,64]{2,1,0:T(2,128)S(1)}) custom-call(bf16[2048,256]{1,0:T(8,128)(2,1)} %bitcast.5, bf16[2048,256]{1,0:T(8,128)(2,1)} %bitcast.6, bf16[2,256,1024]{2,1,0:T(8,128)(2,1)} %wu_hbm.1, bf16[2,1024,256]{2,1,0:T(8,128)(2,1)} %wd_hbm.1, ...), custom_call_target="tpu_custom_call" | custom-call | tf_op jit(solution)/shard_map/blocks/pallas_call | solution.py:512
  55.2 1.4 %store.1 = (bf16[2048,256]{1,0:T(8,128)(2,1)}, f32[2,256,256]{2,1,0:T(8,128)}, f32[2,256,256]{2,1,0:T(8,128)}, f32[7,2,64]{2,1,0:T(2,128)}) custom-call(bf16[2048,256]{1,0:T(8,128)(2,1)S(1)} %get-tuple-element.12.refs_0_, f32[2,256,256]{2,1,0:T(8,128)S(1)} %get-tuple-element.13.refs_1_, f32[2,256,256]{2,1,0:T(8,128)S(1)} %get-tuple-element.14.refs_2_, ...), custom_call_target="tpu_custom_call" | custom-call | tf_op jit(solution)/shard_map/store/pallas_call | solution.py:580
